TPU v7x, 32 devices: a whole 2x2x4 slice. The times are simulated.
32 devices in a mesh: rows: 4 (over z), cols: 8 (over y, x, core).
Axes of the slice: x: 2, y: 2, z: 4, core: 2. Of those that a mesh axis runs over, the one named last changes fastest.
Arguments:
- tokens: bfloat16 [32, 1024, 768], P('rows', 'cols'), may hold values from -6 to 6
- segment_ids: int32 [32, 1024], P('rows'), may hold values from 0 to 3, never falling along the last dimension, each value on 1 to 768 neighbouring positions
- cotangent: bfloat16 [32, 1024, 768], P('rows', 'cols'), may hold values from -6 to 6
- w_qkv: bfloat16 [768, 2304], replicated, may hold values from -0.21875 to 0.21875
- q_bias: float32 [768], replicated, may hold values from -1.2 to 1.2
- v_bias: float32 [768], replicated, may hold values from -1.2 to 1.2
- w_out: bfloat16 [768, 768], replicated, may hold values from -1.75 to 1.75
- out_bias: float32 [768], replicated, may hold values from -1.2 to 1.2
- attn_gain: float32 [768], replicated, may hold values from 0.5 to 1.5
- attn_shift: float32 [768], replicated, may hold values from -1.2 to 1.2
- mlp_gain: float32 [768], replicated, may hold values from 0.5 to 1.5
- mlp_shift: float32 [768], replicated, may hold values from -1.2 to 1.2
- w_up: bfloat16 [768, 3072], replicated, may hold values from -0.21875 to 0.21875
- up_bias: float32 [3072], replicated, may hold values from -1.2 to 1.2
- w_down: bfloat16 [3072, 768], replicated, may hold values from -0.109375 to 0.109375
- down_bias: float32 [768], replicated, may hold values from -1.2 to 1.2
Outputs:
- output: bfloat16 [32, 1024, 768], P('rows', 'cols')
- grad_tokens: float32 [32, 1024, 768], P('rows', 'cols')
- grad_w_qkv: float32 [768, 2304], replicated
- grad_q_bias: float32 [768], replicated
- grad_v_bias: float32 [768], replicated
- grad_w_out: float32 [768, 768], replicated
- grad_out_bias: float32 [768], replicated
- grad_attn_gain: float32 [768], replicated
- grad_attn_shift: float32 [768], replicated
- grad_mlp_gain: float32 [768], replicated
- grad_mlp_shift: float32 [768], replicated
- grad_w_up: float32 [768, 3072], replicated
- grad_up_bias: float32 [3072], replicated
- grad_w_down: float32 [3072, 768], replicated
- grad_down_bias: float32 [768], replicated
Inputs may be any that keep to these rules, and one draw needn't show every extreme that they name: `segment_ids`: along each stored sequence the ids never fall; each document is a run of slots.
All inputs are finite; a program needn't handle non-finite values.
Results may differ from a plain program's by a relative error of at most 0.012.
Values may be sent and summed in bfloat16 or wider, within the bound.
A program may use at most 384 MiB of HBM per device.

v0:
```python
import functools

import jax
import jax.numpy as jnp
from jax import lax
from jax.experimental import pallas as pl
from jax.experimental.pallas import tpu as pltpu
from jax.sharding import PartitionSpec as P

HEADS = 12
HDIM = 64
BF = jnp.bfloat16
F32 = jnp.float32
LOG2E = 1.4426950408889634
BIG = 1e30
BLOCK = 256
MESH = pl.DeviceIdType.MESH
PANEL = 768
SPLIT = 2
STEP = 48
VMEM_LIMIT = 62 * 2**20


def to_whole(value, copies):
    if copies > 1:
        value = jnp.repeat(value, copies, axis=0)
    return lax.all_to_all(value, "cols", 0, 1, tiled=True)


def to_parts(value, copies):
    parts = lax.all_to_all(value, "cols", 1, 0, tiled=True)
    return parts[::copies] if copies > 1 else parts


def dot(a, b, dims=((1,), (0,))):
    return lax.dot_general(a, b, (dims, ((), ())), preferred_element_type=F32)


def norm_parts(values):
    average = jnp.mean(values, axis=-1, keepdims=True)
    centered = values - average
    scale = lax.rsqrt(jnp.mean(centered * centered, axis=-1, keepdims=True) + 1e-05)
    return centered * scale, scale


def norm_back(grad, normal, scale, gain):
    weighted = grad * gain
    inner = jnp.mean(weighted * normal, axis=-1, keepdims=True)
    return scale * (weighted - jnp.mean(weighted, axis=-1, keepdims=True) - normal * inner)


def gelu_tanh(values):
    return jax.nn.gelu(values, approximate=True)


NT=((1,),(1,))

def tri(size, upper):
    r=lax.broadcasted_iota(jnp.int32,(size,size),0); c=lax.broadcasted_iota(jnp.int32,(size,size),1)
    return jnp.where(c>r if upper else c<r, 1.0, 0.0).astype(BF)

def split_sum(mask, x):
    hi=x.astype(BF)
    lo=(x-hi.astype(F32)).astype(BF)
    return dot(mask,hi)+dot(mask,lo)

def lane_low(shape):
    return lax.broadcasted_iota(jnp.int32,shape,1) < HDIM

def attn_fwd_kernel(q_ref,k_ref,v_ref,segc_ref,segr_ref,startr_ref,o_ref,lse_ref,pen_ref):
    L=q_ref.shape[0]; nb=L//BLOCK
    scale=HDIM**-0.5
    pairs=HEADS//2
    upper=tri(BLOCK,True)
    carry=jnp.zeros((1,L),F32)
    for b in range(nb-1,-1,-1):
        i0=b*BLOCK; n=L-i0
        q0=q_ref[i0:i0+BLOCK,0:128]
        q0=jnp.where(lane_low(q0.shape),q0,jnp.zeros_like(q0))
        s=dot(q0,k_ref[i0:L,0:128],NT)*scale
        rows=i0+lax.broadcasted_iota(jnp.int32,(BLOCK,n),0)
        cols=i0+lax.broadcasted_iota(jnp.int32,(BLOCK,n),1)
        same=segc_ref[i0:i0+BLOCK,0:1]==segr_ref[0:1,i0:L]
        picked=same&(cols>rows)&(startr_ref[0:1,i0:L]==0)
        sel=jnp.where(picked,jnp.maximum(s,0.0),0.0)
        if b==nb-1: cin=jnp.zeros((1,n),F32)
        else: cin=jnp.concatenate([jnp.zeros((1,BLOCK),F32),carry],axis=1)
        carried=split_sum(upper,sel)+cin
        pen_ref[i0:i0+BLOCK,i0:L]=jnp.where(same&(cols>=rows),carried*(8.0/L*LOG2E),BIG)
        carry=cin+jnp.sum(sel,axis=0,keepdims=True)
    c=scale*LOG2E
    for b in range(nb):
        i0=b*BLOCK; n=L-i0
        def pair(p,stats,i0=i0,n=n):
            off=pl.multiple_of(p*128,128)
            q=q_ref[i0:i0+BLOCK,pl.ds(off,128)]
            k=k_ref[i0:L,pl.ds(off,128)]
            v=v_ref[i0:L,pl.ds(off,128)]
            low=lane_low(q.shape)
            outs=[]
            lane=lax.broadcasted_iota(jnp.int32,(BLOCK,128),1)
            for h in range(2):
                mine=low if h==0 else jnp.logical_not(low)
                qm=jnp.where(mine,q,jnp.zeros_like(q))
                s=dot(qm,k,NT)*c-pen_ref[i0:i0+BLOCK,i0:L]
                m=jnp.max(s,axis=1,keepdims=True)
                e=jnp.exp2(s-m).astype(BF)
                lowv=lane_low(v.shape)
                vm=jnp.where(lowv if h==0 else jnp.logical_not(lowv),v,jnp.ones_like(v))
                o=dot(e,vm)
                tot=pltpu.roll(o,HDIM,1)
                outs.append(o/tot)
                full=jnp.where(mine,tot,o)
                stats=jnp.where(lane==2*p+h,m+jnp.log2(full),stats)
            o_ref[i0:i0+BLOCK,pl.ds(off,128)]=jnp.where(low,outs[0],outs[1]).astype(BF)
            return stats
        lse_ref[i0:i0+BLOCK,:]=lax.fori_loop(0,pairs,pair,jnp.zeros((BLOCK,128),F32))

def attn_fwd(q,k,v,seg):
    L,D=q.shape
    start=jnp.concatenate([(seg[:-1]!=seg[1:]).astype(jnp.int32),jnp.ones((1,),jnp.int32)])
    vm=pl.BlockSpec(memory_space=pltpu.VMEM)
    return pl.pallas_call(attn_fwd_kernel,
        out_shape=(jax.ShapeDtypeStruct((L,D),BF),jax.ShapeDtypeStruct((L,128),F32),jax.ShapeDtypeStruct((L,L),F32)),
        in_specs=[vm]*6,out_specs=(vm,)*3,
        compiler_params=pltpu.CompilerParams(vmem_limit_bytes=60*2**20),name="attn_fwd")(q,k,v,seg[:,None],seg[None,:],start[None,:])

def attn_bwd_kernel(q_ref,k_ref,v_ref,g_ref,o_ref,lse_ref,pen_ref,startr_ref,out_ref,qt,gt,dkt,dvt,dsum):
    L,D=q_ref.shape; nb=L//BLOCK
    scale=HDIM**-0.5; c=scale*LOG2E
    pairs=HEADS//2
    lower=tri(BLOCK,False)
    for p in range(pairs):
        qt[p*128:(p+1)*128,:]=q_ref[:,p*128:(p+1)*128].T
        gt[p*128:(p+1)*128,:]=g_ref[:,p*128:(p+1)*128].T
    dkt[...]=jnp.zeros_like(dkt); dvt[...]=jnp.zeros_like(dvt)
    carry=jnp.zeros((1,L),F32)
    for b in range(nb):
        i0=b*BLOCK; n=L-i0
        rowsl=slice(i0,i0+BLOCK)
        carry=carry[:,-n:]
        def head(p,h,i0=i0,n=n,rowsl=rowsl):
            static=isinstance(p,int)
            off=p*128 if static else pl.multiple_of(p*128,128)
            q=q_ref[rowsl,pl.ds(off,128)]; g=g_ref[rowsl,pl.ds(off,128)]; o=o_ref[rowsl,pl.ds(off,128)]
            k=k_ref[i0:L,pl.ds(off,128)]; v=v_ref[i0:L,pl.ds(off,128)]
            low=lane_low(q.shape); mine=low if h==0 else jnp.logical_not(low)
            qm=jnp.where(mine,q,jnp.zeros_like(q)); gm=jnp.where(mine,g,jnp.zeros_like(g))
            lane=lax.broadcasted_iota(jnp.int32,(BLOCK,128),1)
            lse=jnp.sum(jnp.where(lane==2*p+h,lse_ref[rowsl,:],0.0),axis=1,keepdims=True)
            delta=jnp.sum(gm.astype(F32)*o.astype(F32),axis=1,keepdims=True)
            s=dot(qm,k,NT)
            pr=jnp.exp2(s*c-pen_ref[rowsl,i0:L]-lse)
            dp=dot(gm,v,NT)
            ds=pr*(dp-delta)
            return s,pr,ds,off,k
        def finish(p,h,pr,ds,off,k,i0=i0,rowsl=rowsl):
            base=p*128+h*HDIM
            if not isinstance(p,int): base=pl.multiple_of(base,64)
            dsb=ds.astype(BF); prb=pr.astype(BF)
            dvt[pl.ds(base,HDIM),i0:L]+=dot(gt[pl.ds(base,HDIM),rowsl],prb)
            dkt[pl.ds(base,HDIM),i0:L]+=dot(qt[pl.ds(base,HDIM),rowsl],dsb)
            return dot(dsb,k)
        dsum[:,i0:L]=jnp.zeros((BLOCK,n),F32)
        def pair(p,carry_):
            dq=[]
            for h in range(2):
                s,pr,ds,off,k=head(p,h)
                dsum[:,i0:L]+=ds
                dq.append(finish(p,h,pr,ds,off,k))
            out_ref[rowsl,pl.ds(off,128)]=(jnp.where(lane_low(dq[0].shape),dq[0],dq[1])*scale).astype(BF)
            return carry_
        lax.fori_loop(1,pairs,pair,0)
        s,pr,ds,off,k=head(0,1)
        dsum[:,i0:L]+=ds
        dq1=finish(0,1,pr,ds,off,k)
        s,pr,ds,off,k=head(0,0)
        total=dsum[:,i0:L]+ds
        rows=i0+lax.broadcasted_iota(jnp.int32,(BLOCK,n),0)
        cols=i0+lax.broadcasted_iota(jnp.int32,(BLOCK,n),1)
        picked=(pen_ref[rowsl,i0:L]<1e29)&(cols>rows)&(startr_ref[0:1,i0:L]==0)&(s>0)
        gsel=(split_sum(lower,total)+carry)*(-8.0/L)
        carry=carry+jnp.sum(total,axis=0,keepdims=True)
        ds=ds+jnp.where(picked,gsel,0.0)
        dq0=finish(0,0,pr,ds,off,k)
        out_ref[rowsl,0:128]=(jnp.where(lane_low(dq0.shape),dq0,dq1)*scale).astype(BF)
    for p in range(pairs):
        sl=slice(p*128,(p+1)*128)
        out_ref[:,D+p*128:D+(p+1)*128]=(dkt[sl,:]*scale).T.astype(BF)
        out_ref[:,2*D+p*128:2*D+(p+1)*128]=dvt[sl,:].T.astype(BF)

def attn_bwd(q,k,v,g,o,lse,pen,seg):
    L,D=q.shape
    start=jnp.concatenate([(seg[:-1]!=seg[1:]).astype(jnp.int32),jnp.ones((1,),jnp.int32)])
    vm=pl.BlockSpec(memory_space=pltpu.VMEM)
    return pl.pallas_call(attn_bwd_kernel,
        out_shape=jax.ShapeDtypeStruct((L,3*D),BF),
        in_specs=[vm]*8,out_specs=vm,
        scratch_shapes=[pltpu.VMEM((D,L),BF),pltpu.VMEM((D,L),BF),pltpu.VMEM((D,L),F32),pltpu.VMEM((D,L),F32),pltpu.VMEM((BLOCK,L),F32)],
        compiler_params=pltpu.CompilerParams(vmem_limit_bytes=60*2**20),name="attn_bwd")(q,k,v,g,o,lse,pen,start[None,:])


def layer(tokens, segs, cotangent, weights, fused):
    (w_qkv, q_bias, v_bias, w_out, out_bias, attn_gain, attn_shift, mlp_gain, mlp_shift,
     w_up, up_bias, w_down, down_bias) = weights
    width = tokens.shape[1]
    inputs = tokens.astype(F32)
    normal_one, scale_one = norm_parts(inputs)
    normed = (normal_one * attn_gain + attn_shift).astype(BF)
    projected = dot(normed, w_qkv)
    queries = (projected[:, :width] + q_bias).astype(BF)
    keys = projected[:, width : 2 * width].astype(BF)
    values = (projected[:, 2 * width :] + v_bias).astype(BF)
    attended, stats, penalty = attn_fwd(queries, keys, values, segs)
    residual = inputs + dot(attended, w_out) + out_bias
    normal_two, scale_two = norm_parts(residual)
    normed_two = (normal_two * mlp_gain + mlp_shift).astype(BF)
    upper = dot(normed_two, w_up) + up_bias
    act, gelu_back = jax.vjp(gelu_tanh, upper)
    act = act.astype(BF)
    output = (residual + dot(act, w_down) + down_bias).astype(BF)
    grad_top = cotangent.astype(F32)
    g_down_bias = jnp.sum(grad_top, axis=0)
    g_w_down = dot(act, cotangent, ((0,), (0,)))
    grad_upper = gelu_back(dot(cotangent, w_down, ((1,), (1,))))[0].astype(BF)
    g_up_bias = jnp.sum(grad_upper.astype(F32), axis=0)
    g_w_up = dot(normed_two, grad_upper, ((0,), (0,)))
    grad_two = dot(grad_upper, w_up, ((1,), (1,)))
    g_mlp_gain = jnp.sum(grad_two * normal_two, axis=0)
    g_mlp_shift = jnp.sum(grad_two, axis=0)
    grad_residual = grad_top + norm_back(grad_two, normal_two, scale_two, mlp_gain)
    grad_branch = grad_residual.astype(BF)
    g_out_bias = jnp.sum(grad_branch.astype(F32), axis=0)
    g_w_out = dot(attended, grad_branch, ((0,), (0,)))
    grad_attended = dot(grad_branch, w_out, ((1,), (1,))).astype(BF)
    if fused:
        grad_attended = lax.optimization_barrier(grad_attended)
        start_sums = jnp.sum((grad_attended.astype(F32) * attended.astype(F32)).reshape(-1, HEADS, HDIM), axis=2)
        delta = jnp.pad(start_sums, ((0, 0), (0, 128 - HEADS)))
        zero = jnp.zeros((width,), F32)
        small = jnp.concatenate([zero, zero, g_out_bias, zero, zero, g_mlp_gain, g_mlp_shift, g_down_bias, g_up_bias])
        small = jnp.pad(small.reshape(-1, width), ((0, 4), (0, 0)))
        return attn_back_and_sums(
            queries, keys, values, grad_attended, delta, stats, segs, tokens, attn_gain, attn_shift, w_qkv, small,
            penalty, grad_residual, g_w_out.astype(BF), g_w_down.astype(BF), g_w_up.astype(BF), output)
    grad_proj = attn_bwd(queries, keys, values, grad_attended, attended, stats, penalty, segs)
    bias_sums = jnp.sum(grad_proj.astype(F32), axis=0)
    g_q_bias = bias_sums[:width]
    g_v_bias = bias_sums[2 * width :]
    g_w_qkv = dot(normed, grad_proj, ((0,), (0,)))
    grad_one = dot(grad_proj, w_qkv, ((1,), (1,)))
    g_attn_gain = jnp.sum(grad_one * normal_one, axis=0)
    g_attn_shift = jnp.sum(grad_one, axis=0)
    grad_tokens = grad_residual + norm_back(grad_one, normal_one, scale_one, attn_gain)
    return output, grad_tokens, (
        g_w_qkv, g_q_bias, g_v_bias, g_w_out, g_out_bias, g_attn_gain, g_attn_shift,
        g_mlp_gain, g_mlp_shift, g_w_up, g_up_bias, g_w_down, g_down_bias)


def view(ref, tall, panel, row, rows, col, cols):
    if tall:
        return ref.at[pl.ds(pl.multiple_of(panel * PANEL + row, 16), rows), pl.ds(col, cols)]
    return ref.at[pl.ds(pl.multiple_of(row, 16), rows), pl.ds(pl.multiple_of(panel * PANEL + col, 128), cols)]


def add_into(dst, row, rows, parts):
    def turn(i, carry):
        at = pl.multiple_of(i * STEP, 16)
        here = pl.ds(pl.multiple_of(row + at, 16), STEP)
        total = dst[here, :].astype(F32)
        for part in parts:
            total = total + part[pl.ds(at, STEP), :].astype(F32)
        dst[here, :] = total.astype(BF)
        return carry

    lax.fori_loop(0, rows // STEP, turn, 0)


def rows_at(ref, row, rows):
    return ref.at[pl.ds(pl.multiple_of(row, 16), rows), :]


def remote(src, dst, sent, landed, device):
    return pltpu.make_async_remote_copy(
        src_ref=src, dst_ref=dst, send_sem=sent, recv_sem=landed, device_id=device, device_id_type=MESH
    )


class Place:
    def __init__(self):
        self.z, self.col = lax.axis_index("rows"), lax.axis_index("cols")
        z, col = self.z, self.col
        self.y, self.x, self.c = col // 4, (col // 2) % 2, col % 2
        y, x, c = self.y, self.x, self.c
        self.core = (z, y * 4 + x * 2 + (1 - c))
        self.across_x = (z, y * 4 + (1 - x) * 2 + c)
        self.across_y = (z, (1 - y) * 4 + x * 2 + c)
        self.along_z = [(lax.rem(z + d, 4), col) for d in range(1, 4)]
        self.along_cols = [(z, lax.rem(col + d, 8)) for d in range(1, 8)]

    def greet(self, devices):
        barrier = pltpu.get_barrier_semaphore()
        for device in devices:
            pl.semaphore_signal(barrier, inc=1, device_id=device, device_id_type=MESH)
        pl.semaphore_wait(barrier, len(devices))


class Chunk:
    def __init__(self, place, n, source, result, tall, first, buffers, sems):
        own, from_core, from_one, from_two, from_z = [b.at[n] for b in buffers]
        sent, landed, local = sems
        width = own.shape[-1]
        x, y, z, c = place.x, place.y, place.z, place.c
        S = lambda k: sent.at[n, k]
        R = lambda k: landed.at[n, k]
        src = lambda panel, row, rows: view(source, tall, panel, row, rows, first, width)
        out = lambda panel, row, rows: view(result, tall, panel, row, rows, first, width)
        near, far = [x, y], [y, x]
        to_near = [place.across_x, place.across_y]
        to_far = [place.across_y, place.across_x]
        half, quarter, piece = PANEL // 2, PANEL // 4, PANEL // 16
        both = range(2)
        self.own, self.from_core, self.from_one = own, from_core, from_one
        self.from_two, self.from_z = from_two, from_z
        self.half, self.quarter, self.piece = half, quarter, piece
        self.keep1 = [near[u] * half for u in both]
        self.send1 = [(1 - near[u]) * half for u in both]
        self.keep2 = [self.keep1[u] + far[u] * quarter for u in both]
        self.send2 = [self.keep1[u] + (1 - far[u]) * quarter for u in both]
        self.last = [self.keep2[u] + z * piece for u in both]
        final = lambda u: rows_at(own.at[u], self.last[u], piece)
        self.load = [pltpu.make_async_copy(src(2 * c + u, 0, PANEL), own.at[u], local.at[n, u]) for u in both]
        self.core = [remote(src(2 * (1 - c) + u, 0, PANEL), from_core.at[u], S(u), R(u), place.core) for u in both]
        self.one = [remote(rows_at(own.at[u], self.send1[u], half), from_one.at[u], S(2 + u), R(2 + u), to_near[u]) for u in both]
        self.two = [remote(rows_at(own.at[u], self.send2[u], quarter), from_two.at[u], S(4 + u), R(4 + u), to_far[u]) for u in both]
        self.deep = [[remote(rows_at(own.at[u], self.keep2[u] + dev[0] * piece, piece), from_z.at[u, d],
                             S(6 + 3 * u + d), R(6 + 3 * u + d), dev)
                      for d, dev in enumerate(place.along_z)] for u in both]
        self.store = [pltpu.make_async_copy(final(u), out(2 * c + u, self.last[u], piece), local.at[n, 2 + u]) for u in both]
        self.deep_back = [[remote(final(u), out(2 * c + u, self.last[u], piece), S(12 + 3 * u + d), R(12 + 3 * u + d), dev)
                           for d, dev in enumerate(place.along_z)] for u in both]
        same = lambda panel, row, rows, k, dev: remote(out(panel, row, rows), out(panel, row, rows), S(k), R(k), dev)
        self.two_back = [same(2 * c + u, self.keep2[u], quarter, 18 + u, to_far[u]) for u in both]
        self.one_back = [same(2 * c + u, self.keep1[u], half, 20 + u, to_near[u]) for u in both]
        self.core_back = [same(2 * c + u, 0, PANEL, 22 + u, place.core) for u in both]

    def begin(self):
        for copy in self.core + self.load:
            copy.start()

    def step(self, k):
        both = range(2)
        own = [self.own.at[u] for u in both]
        if k == 0:
            for u in both:
                self.load[u].wait()
                self.core[u].wait_recv()
                add_into(own[u], self.send1[u], self.half, [rows_at(self.from_core.at[u], self.send1[u], self.half)])
                self.one[u].start()
            for u in both:
                add_into(own[u], self.keep1[u], self.half, [rows_at(self.from_core.at[u], self.keep1[u], self.half)])
        elif k == 1:
            for u in both:
                self.one[u].wait_recv()
                add_into(own[u], self.send2[u], self.quarter, [rows_at(self.from_one.at[u], self.send2[u] - self.keep1[u], self.quarter)])
                self.two[u].start()
                add_into(own[u], self.keep2[u], self.quarter, [rows_at(self.from_one.at[u], self.keep2[u] - self.keep1[u], self.quarter)])
        elif k == 2:
            for u in both:
                self.two[u].wait_recv()
                add_into(own[u], self.keep2[u], self.quarter, [self.from_two.at[u]])
                for copy in self.deep[u]:
                    copy.start()
        elif k == 3:
            for u in both:
                for copy in self.deep[u]:
                    copy.wait_recv()
                add_into(own[u], self.last[u], self.piece, [self.from_z.at[u, d] for d in range(3)])
                for copy in self.deep_back[u]:
                    copy.start()
                self.store[u].start()
        elif k == 4:
            for u in both:
                for copy in self.deep_back[u]:
                    copy.wait_recv()
                self.store[u].wait()
                self.two_back[u].start()
        elif k == 5:
            for u in both:
                self.two_back[u].wait_recv()
                self.one_back[u].start()
        elif k == 6:
            for u in both:
                self.one_back[u].wait_recv()
                self.core_back[u].start()
        else:
            for u in both:
                self.core_back[u].wait_recv()
            for copy in (self.core + self.one + self.two + self.deep[0] + self.deep[1] + self.deep_back[0]
                         + self.deep_back[1] + self.two_back + self.one_back + self.core_back):
                copy.wait_send()


class Timeline:
    LINK = ["core", "plane", "plane", "deep", "deep", "plane", "plane", "core"]
    TAKES = [2.5, 6.0, 3.0, 6.0, 6.0, 3.0, 6.0, 2.5]
    WORK = [2.0, 1.0, 0.5, 0.5, 0.1, 0.1, 0.1, 0.1]

    def __init__(self):
        self.now = 0.0
        self.free = {"core": 0.0, "plane": 0.0, "deep": 0.0}
        self.moving = {}
        self.after_first = {}

    def occupy(self, link, takes):
        self.free[link] = max(self.free[link], self.now) + takes
        return self.free[link] + 1.5

    def begin(self, chunk, then=None):
        chunk.begin()
        self.moving[chunk] = (self.occupy(self.LINK[0], self.TAKES[0]), 0)
        self.after_first[chunk] = then

    def turn(self, chunk):
        done, k = self.moving.pop(chunk)
        self.now = max(self.now, done)
        chunk.step(k)
        self.now += self.WORK[k]
        if k < 7:
            self.moving[chunk] = (self.occupy(self.LINK[k + 1], self.TAKES[k + 1]), k + 1)
        if k == 0 and self.after_first[chunk]:
            self.after_first[chunk]()

    def ready(self):
        while self.moving:
            chunk = min(self.moving, key=lambda c: self.moving[c][0])
            if self.moving[chunk][0] > self.now:
                return
            self.turn(chunk)

    def worked(self, takes):
        self.now += takes
        self.ready()

    def finish(self):
        while self.moving:
            self.turn(min(self.moving, key=lambda c: self.moving[c][0]))


class Homeward:
    def __init__(self, place, source, result, sent, landed, local):
        part = source.shape[0] // 8
        self.copies = [remote(rows_at(source, dev[1] * part, part), result.at[place.col], sent.at[i], landed.at[i], dev)
                       for i, dev in enumerate(place.along_cols)]
        self.own = pltpu.make_async_copy(rows_at(source, place.col * part, part), result.at[place.col], local)

    def start(self):
        for copy in self.copies:
            copy.start()
        self.own.start()

    def wait(self):
        for copy in self.copies:
            copy.wait()
        self.own.wait()


def back_kernel(q_ref, k_ref, v_ref, g_ref, delta_ref, lse_ref, startr_ref, tokens_ref, gain_ref, shift_ref,
                w_ref, small_ref, pen_ref, residual_ref, g_out_ref, down_ref, up_ref, output_ref,
                down_out, up_out, side_out, tokens_out, output_out, small_out,
                qt, gt, dkt, dvt, dsum, pen, dqkv, side, gtok, gres, own, from_core, from_one, from_two, from_z,
                sm_acc, sm_rec, sent, landed, local, home_s, home_r, home_l, sm_s, sm_r, pen_s, res_s, out_s):
    L, D = q_ref.shape
    nb = L // BLOCK
    scale = HDIM**-0.5
    c = scale * LOG2E
    pairs = HEADS // 2
    width = PANEL // SPLIT
    place = Place()
    place.greet(place.along_cols + place.along_z)
    buffers, sems = (own, from_core, from_one, from_two, from_z), (sent, landed, local)
    chunks = []
    for source, result, tall in ((down_ref, down_out, True), (up_ref, up_out, False), (side, side_out, False)):
        for j in range(SPLIT):
            chunks.append(Chunk(place, len(chunks), source, result, tall, j * width, buffers, sems))
    early = 2 * SPLIT
    line = Timeline()

    def chain(n):
        if n < early:
            line.begin(chunks[n], lambda: chain(n + 1))

    chain(0)
    pen_copies = [pltpu.make_async_copy(pen_ref.at[b * BLOCK : (b + 1) * BLOCK, :], pen.at[b % 2], pen_s.at[b % 2]) for b in range(nb)]
    res_copies = [pltpu.make_async_copy(residual_ref.at[b * BLOCK : (b + 1) * BLOCK, :], gres.at[b % 2], res_s.at[b % 2]) for b in range(nb)]
    pen_copies[0].start()
    output_home = Homeward(place, output_ref, output_out, home_s.at[0], home_r.at[0], home_l.at[0])
    output_home.start()
    line.occupy("plane", 16.0)
    out_copy = pltpu.make_async_copy(g_out_ref, side.at[:, 3 * D : 4 * D], out_s)
    out_copy.start()
    for p in range(pairs):
        qt[p * 128 : (p + 1) * 128, :] = q_ref[:, p * 128 : (p + 1) * 128].T
        gt[p * 128 : (p + 1) * 128, :] = g_ref[:, p * 128 : (p + 1) * 128].T
    dkt[...] = jnp.zeros_like(dkt)
    dvt[...] = jnp.zeros_like(dvt)
    line.worked(2.0)
    lower = tri(BLOCK, False)
    carry = jnp.zeros((1, L), F32)
    for b in range(nb):
        i0 = b * BLOCK
        n = L - i0
        rowsl = slice(i0, i0 + BLOCK)
        carry = carry[:, -n:]
        pen_copies[b].wait()
        if b + 1 < nb:
            pen_copies[b + 1].start()
        pen_b = pen.at[b % 2, :, i0:L]

        def head(p, h):
            off = p * 128 if isinstance(p, int) else pl.multiple_of(p * 128, 128)
            q = q_ref[rowsl, pl.ds(off, 128)]
            g = g_ref[rowsl, pl.ds(off, 128)]
            k = k_ref[i0:L, pl.ds(off, 128)]
            v = v_ref[i0:L, pl.ds(off, 128)]
            low = lane_low(q.shape)
            mine = low if h == 0 else jnp.logical_not(low)
            lane = lax.broadcasted_iota(jnp.int32, (BLOCK, 128), 1)
            lse = jnp.sum(jnp.where(lane == 2 * p + h, lse_ref[rowsl, :], 0.0), axis=1, keepdims=True)
            delta = jnp.sum(jnp.where(lane == 2 * p + h, delta_ref[rowsl, :], 0.0), axis=1, keepdims=True)
            s = dot(jnp.where(mine, q, jnp.zeros_like(q)), k, NT)
            pr = jnp.exp2(s * c - pen_b[...] - lse)
            dp = dot(jnp.where(mine, g, jnp.zeros_like(g)), v, NT)
            return s, pr, pr * (dp - delta), off, k

        def finish(p, h, pr, ds, k):
            base = p * 128 + h * HDIM
            if not isinstance(p, int):
                base = pl.multiple_of(base, 64)
            dsb = ds.astype(BF)
            dvt[pl.ds(base, HDIM), i0:L] += dot(gt[pl.ds(base, HDIM), rowsl], pr.astype(BF))
            dkt[pl.ds(base, HDIM), i0:L] += dot(qt[pl.ds(base, HDIM), rowsl], dsb)
            return dot(dsb, k)

        def pair(p, carry_):
            dq = []
            for h in range(2):
                s, pr, ds, off, k = head(p, h)
                dsum[:, i0:L] += ds
                dq.append(finish(p, h, pr, ds, k))
            dqkv[rowsl, pl.ds(off, 128)] = (jnp.where(lane_low(dq[0].shape), dq[0], dq[1]) * scale).astype(BF)
            return carry_

        dsum[:, i0:L] = jnp.zeros((BLOCK, n), F32)
        each = 0.62 * (nb - b)
        for begin, end in ((1, 3), (3, pairs)) if b < 2 else ((1, pairs),):
            lax.fori_loop(begin, end, pair, 0)
            line.worked(each * (end - begin))
        s, pr, ds, off, k = head(0, 1)
        dsum[:, i0:L] += ds
        dq1 = finish(0, 1, pr, ds, k)
        s, pr, ds, off, k = head(0, 0)
        total = dsum[:, i0:L] + ds
        rows = i0 + lax.broadcasted_iota(jnp.int32, (BLOCK, n), 0)
        cols = i0 + lax.broadcasted_iota(jnp.int32, (BLOCK, n), 1)
        picked = (pen_b[...] < 1e29) & (cols > rows) & (startr_ref[0:1, i0:L] == 0) & (s > 0)
        gsel = (split_sum(lower, total) + carry) * (-8.0 / L)
        carry = carry + jnp.sum(total, axis=0, keepdims=True)
        ds = ds + jnp.where(picked, gsel, 0.0)
        dq0 = finish(0, 0, pr, ds, k)
        dqkv[rowsl, 0:128] = (jnp.where(lane_low(dq0.shape), dq0, dq1) * scale).astype(BF)
        line.worked(each * 1.2)
    for p in range(pairs):
        sl = slice(p * 128, (p + 1) * 128)
        dqkv[:, D + p * 128 : D + (p + 1) * 128] = (dkt[sl, :] * scale).T.astype(BF)
        dqkv[:, 2 * D + p * 128 : 2 * D + (p + 1) * 128] = dvt[sl, :].T.astype(BF)

    def normal_of(b):
        values = tokens_ref[b * BLOCK : (b + 1) * BLOCK, :].astype(F32)
        return norm_parts(values)

    for b in range(nb):
        normal, _ = normal_of(b)
        normed = (normal * gain_ref[...] + shift_ref[...]).astype(BF)
        for p in range(pairs):
            qt[p * 128 : (p + 1) * 128, b * BLOCK : (b + 1) * BLOCK] = normed[:, p * 128 : (p + 1) * 128].T
    line.worked(3.0)
    out_copy.wait()
    for j in range(SPLIT):
        for panel in range(3):
            at = slice(panel * D + j * width, panel * D + (j + 1) * width)
            side[:, at] = dot(qt[...], dqkv[:, at]).astype(BF)
        line.now += 2.5
        line.begin(chunks[early + j])
        line.ready()
    sm_acc[0] = small_ref[...]
    sm_acc[0, 0:1, :] = jnp.sum(dqkv[:, 0:D].astype(F32), axis=0, keepdims=True)
    sm_acc[0, 1:2, :] = jnp.sum(dqkv[:, 2 * D : 3 * D].astype(F32), axis=0, keepdims=True)
    res_copies[0].start()
    g_gain = jnp.zeros((1, D), F32)
    g_shift = jnp.zeros((1, D), F32)
    for b in range(nb):
        rowsl = slice(b * BLOCK, (b + 1) * BLOCK)
        if b + 1 < nb:
            res_copies[b + 1].start()
        normal, spread = normal_of(b)
        grad = dot(dqkv[rowsl, :], w_ref[...], NT)
        g_gain = g_gain + jnp.sum(grad * normal, axis=0, keepdims=True)
        g_shift = g_shift + jnp.sum(grad, axis=0, keepdims=True)
        back = norm_back(grad, normal, spread, gain_ref[...])
        res_copies[b].wait()
        gtok[rowsl, :] = (gres[b % 2] + back).astype(BF)
        line.worked(3.0)
    tokens_home = Homeward(place, gtok, tokens_out, home_s.at[1], home_r.at[1], home_l.at[1])
    tokens_home.start()
    line.occupy("plane", 16.0)
    sm_acc[0, 3:4, :] = g_gain
    sm_acc[0, 4:5, :] = g_shift
    z, col = place.z, place.col
    friends = [place.core, place.across_x, place.across_y, (z + 1 - 2 * (z % 2), col), (lax.rem(z + 2, 4), col)]
    smalls = [remote(sm_acc.at[i], sm_rec.at[i], sm_s.at[i], sm_r.at[i], friends[i]) for i in range(5)]
    smalls[0].start()
    for i in range(5):
        line.worked(4.0)
        smalls[i].wait_recv()
        following = sm_acc[i] + sm_rec[i]
        if i < 4:
            sm_acc[i + 1] = following
            smalls[i + 1].start()
        else:
            small_out[...] = following
    line.finish()
    for copy in smalls:
        copy.wait_send()
    output_home.wait()
    tokens_home.wait()


def attn_back_and_sums(q, k, v, g, delta, lse, seg, tokens, gain, shift, w_qkv, small, pen, residual, g_out, down, up, output):
    L, D = q.shape
    start = jnp.concatenate([(seg[:-1] != seg[1:]).astype(jnp.int32), jnp.ones((1,), jnp.int32)])
    N, W = 3 * SPLIT, PANEL // SPLIT
    hbm = pl.BlockSpec(memory_space=pl.ANY)
    vm = pl.BlockSpec(memory_space=pltpu.VMEM)
    dma = pltpu.SemaphoreType.DMA
    shape = jax.ShapeDtypeStruct
    return pl.pallas_call(
        back_kernel,
        out_shape=(shape(down.shape, BF), shape(up.shape, BF), shape((D, 4 * D), BF),
                   shape((8, L // 8, D), BF), shape((8, L // 8, D), BF), shape(small.shape, F32)),
        in_specs=[vm] * 12 + [hbm] * 6,
        out_specs=(hbm,) * 5 + (vm,),
        scratch_shapes=[
            pltpu.VMEM((D, L), BF), pltpu.VMEM((D, L), BF), pltpu.VMEM((D, L), F32), pltpu.VMEM((D, L), F32),
            pltpu.VMEM((BLOCK, L), F32), pltpu.VMEM((2, BLOCK, L), F32), pltpu.VMEM((L, 3 * D), BF),
            pltpu.VMEM((D, 4 * D), BF), pltpu.VMEM((L, D), BF), pltpu.VMEM((2, BLOCK, D), F32),
            pltpu.VMEM((N, 2, PANEL, W), BF), pltpu.VMEM((N, 2, PANEL, W), BF), pltpu.VMEM((N, 2, PANEL // 2, W), BF),
            pltpu.VMEM((N, 2, PANEL // 4, W), BF), pltpu.VMEM((N, 2, 3, PANEL // 16, W), BF),
            pltpu.VMEM((5,) + small.shape, F32), pltpu.VMEM((5,) + small.shape, F32),
            dma((N, 24)), dma((N, 24)), dma((N, 4)), dma((2, 7)), dma((2, 7)), dma((2,)), dma((5,)), dma((5,)),
            dma((2,)), dma((2,)), dma,
        ],
        compiler_params=pltpu.CompilerParams(vmem_limit_bytes=VMEM_LIMIT, collective_id=1, has_side_effects=True),
        name="attn_back_and_sums",
    )(q, k, v, g, delta, lse, start[None, :], tokens, gain[None, :], shift[None, :], w_qkv, small, pen, residual, g_out, down, up, output)


def summed_grads(grads, copies):
    grads = [g / copies for g in grads]
    matrices = [i for i, g in enumerate(grads) if g.ndim == 2]
    vectors = [i for i, g in enumerate(grads) if g.ndim == 1]
    big = lax.psum([grads[i].astype(BF) for i in matrices], ("rows", "cols"))
    small = lax.psum(jnp.concatenate([grads[i] for i in vectors]), ("rows", "cols"))
    out = [None] * len(grads)
    for i, g in zip(matrices, big):
        out[i] = g.astype(F32)
    at = 0
    for i in vectors:
        out[i] = small[at : at + grads[i].shape[0]]
        at += grads[i].shape[0]
    return out


def whole_by_permutes(value):
    parts, cols = value.shape[0], lax.axis_size("cols")
    me = lax.axis_index("cols")
    whole = jnp.zeros_like(value)
    own = lax.dynamic_slice_in_dim(value, me, 1, 0)
    whole = lax.dynamic_update_slice_in_dim(whole, own, me, 0)
    for step in range(1, cols):
        block = lax.dynamic_slice_in_dim(value, lax.rem(me + step, cols), 1, 0)
        block = lax.ppermute(block, "cols", [(i, (i + step) % cols) for i in range(cols)])
        whole = lax.dynamic_update_slice_in_dim(whole, block, lax.rem(me - step + cols, cols), 0)
    return whole


def per_device(tokens, segment_ids, cotangent, *weights):
    seqs, part, width = tokens.shape
    cols = lax.axis_size("cols")
    fitting = (lax.axis_size("rows"), cols, seqs) == (4, 8, 8)
    copies = max(1, cols // seqs)
    held = max(1, seqs // cols)
    first = (lax.axis_index("cols") // copies) * held
    segs = lax.dynamic_slice_in_dim(segment_ids, first, held, 0)
    tokens_whole = to_whole(tokens, copies)
    if fitting:
        cotangent_whole = whole_by_permutes(cotangent).reshape(1, -1, width)
    else:
        cotangent_whole = to_whole(cotangent, copies)
    if fitting:
        down, up, side, grad_tokens, output, small = layer(tokens_whole[0], segs[0], cotangent_whole[0], weights, True)
        return (
            output, grad_tokens.astype(F32), side[:, : 3 * width].astype(F32), small[0], small[1],
            side[:, 3 * width :].astype(F32), small[2], small[3], small[4], small[5], small[6],
            up.astype(F32), small[8:12].reshape(-1), down.astype(F32), small[7])
    results = [
        layer(tokens_whole[s], segs[s], cotangent_whole[s], weights, False) for s in range(held)
    ]
    output = jnp.stack([r[0] for r in results])
    grad_tokens = jnp.stack([r[1] for r in results])
    grads = [sum(parts[1:], parts[0]) for parts in zip(*[r[2] for r in results])]
    return (
        to_parts(output, copies),
        to_parts(grad_tokens.astype(BF), copies).astype(F32),
        *summed_grads(grads, copies),
    )


def solution(mesh):
    placed = (P("rows", "cols", None), P("rows", None), P("rows", "cols", None)) + (P(),) * 13
    return jax.shard_map(
        per_device,
        mesh=mesh,
        in_specs=placed,
        out_specs=(P("rows", "cols", None), P("rows", "cols", None)) + (P(),) * 13,
        check_vma=False,
    )
```

profile of v0, /device:TPU:0, one launch (start us, length us, event | category | flops | bytes accessed | tf_op | source)
XLA Modules:
  0.0 393.6 jit_solution(16849362963626309593)
XLA Ops:
  0.7 5.4 %all-to-all-start = ((bf16[8,128,768]{2,1,0:T(8,128)(2,1)}), bf16[8,128,768]{2,1,0:T(8,128)(2,1)}, u32[]{:S(2)}, u32[]{:S(2)}) async-start(bf16[8,128,768]{2,1,0:T(8,128)(2,1)} %param.16), calls=%async_computation | async-start | bytes 3145728 | tf_op jit(solution)/shard_map/all_to_all | solution.py:27
  6.2 1.3 broadcast_in_dim.10
  7.4 0.9 constant_dynamic-slice_fusion.2
  8.4 2.6 collective-permute-start.6
  11.5 1.0 collective-permute-start.1
  13.1 0.8 fusion.40
  15.0 1.0 copy.35.segc_ref
  16.1 0.9 compare_reduce_fusion
  17.0 1.3 constant_dynamic-update-slice_fusion.13
  18.3 1.4 constant_dynamic-slice_fusion.1.segr_ref
  20.3 17.5 %collective-permute-done = bf16[1,128,768]{2,1,0:T(8,128)(2,1)S(1)} collective-permute-done((bf16[1,128,768]{2,1,0:T(8,128)(2,1)}, bf16[1,128,768]{2,1,0:T(8,128)(2,1)S(1)}, u32[]{:S(2)}, u32[]{:S(2)}) %collective-permute-start) | collective-permute-done | bytes 196640 | tf_op jit(solution)/shard_map/ppermute | solution.py:692
  37.8 0.7 constant_dynamic-update-slice_fusion.6
  39.7 4.6 %collective-permute-done.2 = bf16[1,128,768]{2,1,0:T(8,128)(2,1)S(1)} collective-permute-done((bf16[1,128,768]{2,1,0:T(8,128)(2,1)}, bf16[1,128,768]{2,1,0:T(8,128)(2,1)S(1)}, u32[]{:S(2)}, u32[]{:S(2)}) %collective-permute-start.2) | collective-permute-done | bytes 196640 | tf_op jit(solution)/shard_map/ppermute | solution.py:692
  44.3 0.7 constant_dynamic-update-slice_fusion.4
  45.0 0.7 constant_dynamic-update-slice_fusion.3
  45.7 0.7 constant_dynamic-update-slice_fusion.2
  46.4 0.7 constant_dynamic-update-slice_fusion.1
  47.1 0.7 constant_dynamic-update-slice_fusion
  47.8 1.7 convert_reduce_fusion.2
  49.4 1.7 convert_reduce_fusion.1
  51.1 2.0 fusion.13
  53.1 6.6 %fusion.16 = f32[1024,2304]{1,0:T(8,128)S(1)} fusion(bf16[768,2304]{1,0:T(8,128)(2,1)} %w_ref.1, bf16[1024,768]{1,0:T(8,128)(2,1)} %bitcast.tokens_ref, f32[768]{0:T(1024)S(1)} %copy-done.11, f32[768]{0:T(1024)S(1)} %copy-done.12, f32[1024]{0:T(1024)S(1)} %rsqrt_bitcast_fusion, f32[1024]{0:T(1024)S(1)} %get-tuple-element.57), kind=kOutput, calls=%fused_computation.42 | convolution fusion | flops 3628597248 | bytes 14563328 | tf_op jit(solution)/shard_map/dot_general | solution.py:36
  59.8 1.3 slice.89.k_ref
  61.1 2.3 fusion.14
  63.4 31.0 %attn_fwd.1 = (bf16[1024,768]{1,0:T(8,128)(2,1)}, f32[1024,128]{1,0:T(8,128)}, f32[1024,1024]{1,0:T(8,128)}) custom-call(bf16[1024,768]{1,0:T(8,128)(2,1)} %get-tuple-element.48.q_ref, bf16[1024,768]{1,0:T(8,128)(2,1)} %slice.89.k_ref, bf16[1024,768]{1,0:T(8,128)(2,1)} %get-tuple-element.47.v_ref, s32[1024,1]{1,0:T(8,128)} %copy.35.segc_ref, ...), custom_call_target="tpu_custom_call" | custom-call | tf_op jit(solution)/shard_map/attn_fwd/pallas_call | solution.py:123
  94.4 3.6 fusion.26
  98.7 8.3 %fusion.25 = f32[1024,3072]{1,0:T(8,128)} fusion(bf16[768,3072]{1,0:T(8,128)(2,1)S(1)} %bitcast.31, f32[1024,768]{1,0:T(8,128)S(1)} %get-tuple-element.60, f32[768]{0:T(1024)S(1)} %copy-done.15, f32[768]{0:T(1024)S(1)} %copy-done.10, f32[1024]{0:T(1024)S(1)} %add_rsqrt_fusion, f32[1024]{0:T(1024)S(1)} %broadcast_multiply_fusion.2), kind=kOutput, calls=%fused_computation.92 | convolution fusion | flops 4835770368 | bytes 20461568 | tf_op jit(solution)/shard_map/dot_general | solution.py:36
  107.0 12.6 %convolution_convert_fusion.1.down_ref = bf16[3072,768]{1,0:T(8,128)(2,1)} fusion(bf16[1024,768]{1,0:T(8,128)(2,1)} %bitcast.3, f32[1024,3072]{1,0:T(8,128)} %fusion.25, f32[3072]{0:T(1024)S(1)} %copy-done.13), kind=kOutput, calls=%fused_computation.12 | convolution fusion | flops 4865654784 | bytes 18886656 | tf_op jit(solution)/shard_map/dot_general | solution.py:36
  119.6 17.0 %convert_reduce_fusion = (f32[3072]{0:T(1024)S(1)}, bf16[1024,3072]{1,0:T(8,128)(2,1)}) fusion(f32[1024,3072]{1,0:T(8,128)} %fusion.25, f32[3072]{0:T(1024)S(1)} %copy-done.13, bf16[1024,768]{1,0:T(8,128)(2,1)} %bitcast.3, bf16[3072,768]{1,0:T(8,128)(2,1)S(1)} %bitcast.33), kind=kOutput, calls=%fused_computation.10 | convolution fusion | flops 4904186880 | bytes 25190400 | tf_op jit(solution)/shard_map/dot_general | solution.py:36
  136.6 8.0 %multiply_reduce_fusion = (f32[768]{0:T(1024)S(1)}, f32[1024]{0:T(1024)S(1)}, f32[1024]{0:T(1024)S(1)}, f32[768]{0:T(1024)S(1)}, f32[1024,768]{1,0:T(8,128)S(1)}) fusion(f32[1024,768]{1,0:T(8,128)S(1)} %get-tuple-element.60, f32[1024]{0:T(1024)S(1)} %add_rsqrt_fusion, f32[1024]{0:T(1024)S(1)} %broadcast_multiply_fusion.2, f32[768]{0:T(1024)S(1)} %copy-done.10, ...), kind=kOutput, calls=%fused_computation.32 | convolution fusion | flops 4838912000 | bytes 17327104 | tf_op jit(solution)/shard_map/dot_general | solution.py:36
  144.6 9.9 %convolution_convert_fusion.up_ref = bf16[768,3072]{1,0:T(8,128)(2,1)} fusion(bf16[1024,3072]{1,0:T(8,128)(2,1)} %get-tuple-element.63, f32[1024,768]{1,0:T(8,128)S(1)} %get-tuple-element.60, f32[768]{0:T(1024)S(1)} %copy-done.15, f32[768]{0:T(1024)S(1)} %copy-done.10, f32[1024]{0:T(1024)S(1)} %add_rsqrt_fusion, f32[1024]{0:T(1024)S(1)} %broadcast_multiply_fusion.2), kind=kOutput, calls=%fused_computation.11 | convolution fusion | flops 4838129664 | bytes 14170112 | tf_op jit(solution)/shard_map/dot_general | solution.py:36
  154.5 2.6 convert_reduce_fusion.3
  157.2 2.5 convolution_convert_fusion.3.g_out_ref
  159.7 1.5 convolution_convert_fusion.2.g_ref
  161.2 12.3 %add_convert_fusion.output_ref = bf16[1024,768]{1,0:T(8,128)(2,1)} fusion(f32[1024,768]{1,0:T(8,128)S(1)} %get-tuple-element.60, bf16[3072,768]{1,0:T(8,128)(2,1)S(1)} %bitcast.33, f32[768]{0:T(1024)S(1)} %copy-done.16, f32[1024,3072]{1,0:T(8,128)} %fusion.25, f32[3072]{0:T(1024)S(1)} %copy-done.13), kind=kOutput, calls=%fused_computation.30 | convolution fusion | flops 4865654784 | bytes 22035456 | tf_op jit(solution)/shard_map/dot_general | solution.py:36
  173.6 3.4 convert_multiply_fusion
  176.9 3.5 copy.37
  181.1 2.3 reduce_sum.114
  183.6 0.8 pad.8.delta_ref
  184.4 181.6 %attn_back_and_sums.1 = (bf16[3072,768]{1,0:T(8,128)(2,1)}, bf16[768,3072]{1,0:T(8,128)(2,1)}, bf16[768,3072]{1,0:T(8,128)(2,1)}, bf16[8,128,768]{2,1,0:T(8,128)...) custom-call(bf16[1024,768]{1,0:T(8,128)(2,1)} %get-tuple-element.48.q_ref, bf16[1024,768]{1,0:T(8,128)(2,1)} %slice.89.k_ref, ...), custom_call_target="tpu_custom_call" | custom-call | tf_op jit(solution)/shard_map/attn_back_and_sums/pallas_call | solution.py:647
  366.0 0.7 slice.67
  366.8 1.9 slice_reduce_fusion
  368.7 2.8 slice_convert_fusion.2
  371.5 5.6 %slice_convert_fusion = f32[768,2304]{1,0:T(8,128)} fusion(bf16[768,3072]{1,0:T(8,128)(2,1)} %get-tuple-element.29), kind=kLoop, calls=%fused_computation.17 | loop fusion | flops 1769472 | bytes 10616832 | tf_op jit(solution)/shard_map/convert_element_type | solution.py:713
  377.7 1.9 convert_element_type.108
  379.7 7.8 %convert_element_type.111 = f32[768,3072]{1,0:T(8,128)} convert(bf16[768,3072]{1,0:T(8,128)(2,1)} %get-tuple-element.31) | non-fusion elementwise | flops 2359296 | bytes 14155776 | tf_op jit(solution)/shard_map/convert_element_type | solution.py:715
  387.5 4.5 %convert_element_type.112 = f32[3072,768]{1,0:T(8,128)} convert(bf16[3072,768]{1,0:T(8,128)(2,1)S(1)} %bitcast.27) | non-fusion elementwise | flops 2359296 | bytes 14155776 | tf_op jit(solution)/shard_map/convert_element_type | solution.py:715
  392.0 1.1 copy.56
  (81 shorter events, 6.4 us)
Async XLA Ops:
  0.6 93.7 %copy-start = (bf16[768,768]{1,0:T(8,128)(2,1)S(1)}, bf16[768,768]{1,0:T(8,128)(2,1)}, u32[]{:S(2)}) copy-start(bf16[768,768]{1,0:T(8,128)(2,1)} %param.22) | copy-start | bytes 3538948
  0.7 6.8 %copy-start.3 = (bf16[8,128,768]{2,1,0:T(8,128)(2,1)S(1)}, bf16[8,128,768]{2,1,0:T(8,128)(2,1)}, u32[]{:S(2)}) copy-start(bf16[8,128,768]{2,1,0:T(8,128)(2,1)} %param.18) | copy-start | bytes 4718596
  0.7 48.8 %all-to-all-start = ((bf16[8,128,768]{2,1,0:T(8,128)(2,1)}), bf16[8,128,768]{2,1,0:T(8,128)(2,1)}, u32[]{:S(2)}, u32[]{:S(2)}) async-start(bf16[8,128,768]{2,1,0:T(8,128)(2,1)} %param.16), calls=%async_computation | async-start | bytes 3145728 | tf_op jit(solution)/shard_map/all_to_all | solution.py:27
  6.1 7.8 %copy-start.12 = (f32[768]{0:T(1024)S(1)}, f32[768]{0:T(1024)}, u32[]{:S(2)}) copy-start(f32[768]{0:T(1024)} %param.24) | copy-start | bytes 9220
  6.1 8.3 %copy-start.11 = (f32[768]{0:T(1024)S(1)}, f32[768]{0:T(1024)}, u32[]{:S(2)}) copy-start(f32[768]{0:T(1024)} %param.25) | copy-start | bytes 9220
  8.4 38.7 %collective-permute-start.6 = (bf16[1,128,768]{2,1,0:T(8,128)(2,1)S(1)}, bf16[1,128,768]{2,1,0:T(8,128)(2,1)S(1)}, u32[]{:S(2)}, u32[]{:S(2)}) collective-permute-start(bf16[1,128,768]{2,1,0:T(8,128)(2,1)S(1)} %get-tuple-element.49), channel_id=1, source_target_pairs={{0,7},{1,0},{2,1},{3,2},{4,3},{5,4},{6,5},{7,6},{8,15},{9,8},{10,9... | collective-permute-start | bytes 589832 | tf_op jit(solution)/shard_map/ppermute | solution.py:692
  11.0 34.7 %collective-permute-start.4 = (bf16[1,128,768]{2,1,0:T(8,128)(2,1)S(1)}, bf16[1,128,768]{2,1,0:T(8,128)(2,1)S(1)}, u32[]{:S(2)}, u32[]{:S(2)}) collective-permute-start(bf16[1,128,768]{2,1,0:T(8,128)(2,1)S(1)} %get-tuple-element.50), channel_id=1, source_target_pairs={{0,5},{1,6},{2,7},{3,0},{4,1},{5,2},{6,3},{7,4},{8,13},{9,14},{10,... | collective-permute-start | bytes 589832 | tf_op jit(solution)/shard_map/ppermute | solution.py:692
  11.0 34.0 %collective-permute-start.3 = (bf16[1,128,768]{2,1,0:T(8,128)(2,1)S(1)}, bf16[1,128,768]{2,1,0:T(8,128)(2,1)S(1)}, u32[]{:S(2)}, u32[]{:S(2)}) collective-permute-start(bf16[1,128,768]{2,1,0:T(8,128)(2,1)S(1)} %get-tuple-element.51), channel_id=1, source_target_pairs={{0,4},{1,5},{2,6},{3,7},{4,0},{5,1},{6,2},{7,3},{8,12},{9,13},{10,... | collective-permute-start | bytes 589832 | tf_op jit(solution)/shard_map/ppermute | solution.py:692
  11.5 27.0 %collective-permute-start.1 = (bf16[1,128,768]{2,1,0:T(8,128)(2,1)}, bf16[1,128,768]{2,1,0:T(8,128)(2,1)S(1)}, u32[]{:S(2)}, u32[]{:S(2)}) collective-permute-start(bf16[1,128,768]{2,1,0:T(8,128)(2,1)} %get-tuple-element.53), channel_id=1, source_target_pairs={{0,2},{1,3},{2,4},{3,5},{4,6},{5,7},{6,0},{7,1},{8,10},{9,11},{10,... | collective-permute-start | bytes 589832 | tf_op jit(solution)/shard_map/ppermute | solution.py:692
  12.5 25.3 %collective-permute-start = (bf16[1,128,768]{2,1,0:T(8,128)(2,1)}, bf16[1,128,768]{2,1,0:T(8,128)(2,1)S(1)}, u32[]{:S(2)}, u32[]{:S(2)}) collective-permute-start(bf16[1,128,768]{2,1,0:T(8,128)(2,1)} %get-tuple-element.54), channel_id=1, source_target_pairs={{0,1},{1,2},{2,3},{3,4},{4,5},{5,6},{6,7},{7,0},{8,9},{9,10},{10,1... | collective-permute-start | bytes 589832 | tf_op jit(solution)/shard_map/ppermute | solution.py:692
  37.8 6.5 %collective-permute-start.2 = (bf16[1,128,768]{2,1,0:T(8,128)(2,1)}, bf16[1,128,768]{2,1,0:T(8,128)(2,1)S(1)}, u32[]{:S(2)}, u32[]{:S(2)}) collective-permute-start(bf16[1,128,768]{2,1,0:T(8,128)(2,1)} %get-tuple-element.52), channel_id=1, source_target_pairs={{0,3},{1,4},{2,5},{3,6},{4,7},{5,0},{6,1},{7,2},{8,11},{9,12},{10,... | collective-permute-start | bytes 589832 | tf_op jit(solution)/shard_map/ppermute | solution.py:692
  38.5 7.8 %collective-permute-start.5 = (bf16[1,128,768]{2,1,0:T(8,128)(2,1)S(1)}, bf16[1,128,768]{2,1,0:T(8,128)(2,1)S(1)}, u32[]{:S(2)}, u32[]{:S(2)}) collective-permute-start(bf16[1,128,768]{2,1,0:T(8,128)(2,1)S(1)} %get-tuple-element.56), channel_id=1, source_target_pairs={{0,6},{1,7},{2,0},{3,1},{4,2},{5,3},{6,4},{7,5},{8,14},{9,15},{10,... | collective-permute-start | bytes 589832 | tf_op jit(solution)/shard_map/ppermute | solution.py:692
  59.8 1.3 copy-start.8
  59.8 1.3 copy-start.9
  63.4 31.0 %copy-start.14 = (f32[768]{0:T(1024)S(1)}, f32[768]{0:T(1024)}, u32[]{:S(2)}) copy-start(f32[768]{0:T(1024)} %param.23) | copy-start | bytes 9220
  94.4 4.2 %slice-start.2 = ((s8[4718592]{0:T(1024)(128)(4,1)}), s8[4194304]{0:T(1024)(128)(4,1)S(1)}, s32[]{:S(2)}) async-start(s8[4718592]{0:T(1024)(128)(4,1)} %bitcast.30), calls=%async_computation.3 | async-start | bytes 8388608
  94.4 4.2 %slice-start.3 = ((s8[4718592]{0:T(1024)(128)(4,1)}), s8[524288]{0:T(1024)(128)(4,1)S(1)}, s32[]{:S(2)}) async-start(s8[4718592]{0:T(1024)(128)(4,1)} %bitcast.30), calls=%async_computation.4 | async-start | bytes 1048576
  97.9 0.7 copy-start.10
  98.0 0.7 copy-start.15
  98.7 8.3 %copy-start.13 = (f32[3072]{0:T(1024)S(1)}, f32[3072]{0:T(1024)}, u32[]{:S(2)}) copy-start(f32[3072]{0:T(1024)} %param.29) | copy-start | bytes 36868
  98.7 21.0 %slice-start.4 = ((s8[4718592]{0:T(1024)(128)(4,1)}), s8[4194304]{0:T(1024)(128)(4,1)S(1)}, s32[]{:S(2)}) async-start(s8[4718592]{0:T(1024)(128)(4,1)} %bitcast.32), calls=%async_computation.5 | async-start | bytes 8388608
  107.0 12.6 %slice-start.5 = ((s8[4718592]{0:T(1024)(128)(4,1)}), s8[524288]{0:T(1024)(128)(4,1)S(1)}, s32[]{:S(2)}) async-start(s8[4718592]{0:T(1024)(128)(4,1)} %bitcast.32), calls=%async_computation.6 | async-start | bytes 1048576
  154.5 2.6 copy-start.5
  157.1 2.5 copy-start.1
  159.7 1.5 copy-start.16
  161.1 12.4 %copy-start.2 = (bf16[1024,768]{1,0:T(8,128)(2,1)}, bf16[1024,768]{1,0:T(8,128)(2,1)S(1)}, u32[]{:S(2)}) copy-start(bf16[1024,768]{1,0:T(8,128)(2,1)S(1)} %convolution_convert_fusion.2.g_ref) | copy-start | bytes 4718596
  161.2 12.3 %copy-start.7 = (f32[9216]{0:T(1024)S(1)}, f32[9216]{0:T(1024)}, u32[]{:S(2)}) copy-start(f32[9216]{0:T(1024)} %constant_dynamic-update-slice_fusion.13) | copy-start | bytes 110596
  371.5 6.2 %copy-start.6 = (bf16[8,128,768]{2,1,0:T(8,128)(2,1)S(1)}, bf16[8,128,768]{2,1,0:T(8,128)(2,1)}, u32[]{:S(2)}) copy-start(bf16[8,128,768]{2,1,0:T(8,128)(2,1)} %get-tuple-element.28) | copy-start | bytes 4718596
  377.7 9.8 %slice-start = ((s8[4718592]{0:T(1024)(128)(4,1)}), s8[4194304]{0:T(1024)(128)(4,1)S(1)}, s32[]{:S(2)}) async-start(s8[4718592]{0:T(1024)(128)(4,1)} %bitcast.26), calls=%async_computation.1 | async-start | bytes 8388608
  379.7 7.8 %slice-start.1 = ((s8[4718592]{0:T(1024)(128)(4,1)}), s8[524288]{0:T(1024)(128)(4,1)S(1)}, s32[]{:S(2)}) async-start(s8[4718592]{0:T(1024)(128)(4,1)} %bitcast.26), calls=%async_computation.2 | async-start | bytes 1048576
  387.5 4.5 %copy-start.4 = (bf16[8,128,768]{2,1,0:T(8,128)(2,1)S(1)}, bf16[8,128,768]{2,1,0:T(8,128)(2,1)}, u32[]{:S(2)}) copy-start(bf16[8,128,768]{2,1,0:T(8,128)(2,1)} %get-tuple-element.81) | copy-start | bytes 4718596
where the time goes:
time: 401 us; the launch traced here: 394 us
  Pallas kernels  213 us (53%)
  matrix products  82.3 us (21%)
  other arithmetic  40.7 us (10%)
  local copies, waits for them, and re-layouts  23.8 us (6%)
  waiting for transfers between devices  22.1 us (6%)
  starting transfers between devices  10.7 us (3%)
    pallas_call x1, Pallas kernels, attn_back_and_sums(): pl.pallas_call(back_kernel, out_shape=(shape(down.shape, BF), shape(up.sh...  182 us
    dot_general x10, matrix products, dot(): return lax.dot_general(a, b, (dims, ((), ())), preferred_element_type=F32)  82.3 us
    pallas_call x1, Pallas kernels, attn_fwd(): pl.pallas_call(attn_fwd_kernel, out_shape=(jax.ShapeDtypeStruct((L, D), B...  31 us
    ppermute x7, waiting for transfers between devices, whole_by_permutes(): lax.ppermute(block, 'cols', [(i, (i + step) % cols) for i in range(cols)])  22.1 us
  transfers between devices with their start and end apart: 8, of which 2 were waited for; matrix products, arithmetic and copies ran while one was open for 4% of the time, Pallas kernels for 0%

commit v1 on v0

--- a/solution.py
+++ b/solution.py
@@ -18,6 +18,7 @@
 PANEL = 768
 SPLIT = 2
 STEP = 48
+ROWS = 256
 VMEM_LIMIT = 62 * 2**20
 
 
@@ -67,63 +68,86 @@
 def lane_low(shape):
     return lax.broadcasted_iota(jnp.int32,shape,1) < HDIM
 
-def attn_fwd_kernel(q_ref,k_ref,v_ref,segc_ref,segr_ref,startr_ref,o_ref,lse_ref,pen_ref):
-    L=q_ref.shape[0]; nb=L//BLOCK
-    scale=HDIM**-0.5
-    pairs=HEADS//2
-    upper=tri(BLOCK,True)
-    carry=jnp.zeros((1,L),F32)
-    for b in range(nb-1,-1,-1):
-        i0=b*BLOCK; n=L-i0
-        q0=q_ref[i0:i0+BLOCK,0:128]
-        q0=jnp.where(lane_low(q0.shape),q0,jnp.zeros_like(q0))
-        s=dot(q0,k_ref[i0:L,0:128],NT)*scale
-        rows=i0+lax.broadcasted_iota(jnp.int32,(BLOCK,n),0)
-        cols=i0+lax.broadcasted_iota(jnp.int32,(BLOCK,n),1)
-        same=segc_ref[i0:i0+BLOCK,0:1]==segr_ref[0:1,i0:L]
-        picked=same&(cols>rows)&(startr_ref[0:1,i0:L]==0)
-        sel=jnp.where(picked,jnp.maximum(s,0.0),0.0)
-        if b==nb-1: cin=jnp.zeros((1,n),F32)
-        else: cin=jnp.concatenate([jnp.zeros((1,BLOCK),F32),carry],axis=1)
-        carried=split_sum(upper,sel)+cin
-        pen_ref[i0:i0+BLOCK,i0:L]=jnp.where(same&(cols>=rows),carried*(8.0/L*LOG2E),BIG)
-        carry=cin+jnp.sum(sel,axis=0,keepdims=True)
-    c=scale*LOG2E
+def seg_column(segr_ref, i0):
+    shape = (BLOCK, BLOCK)
+    same = lax.broadcasted_iota(jnp.int32, shape, 0) == lax.broadcasted_iota(jnp.int32, shape, 1)
+    ids = segr_ref[0:1, i0 : i0 + BLOCK].astype(F32)
+    return jnp.sum(jnp.where(same, ids, 0.0), axis=1, keepdims=True).astype(jnp.int32)
+
+
+def attend(q_ref, k_ref, v_ref, seg_ref, o_ref, lse_ref, pen_ref):
+    segr_ref, startr_ref = seg_ref.at[0:1], seg_ref.at[1:2]
+    L = q_ref.shape[0]
+    nb = L // BLOCK
+    scale = HDIM**-0.5
+    upper = tri(BLOCK, True)
+    carry = jnp.zeros((1, L), F32)
+    for b in range(nb - 1, -1, -1):
+        i0 = b * BLOCK
+        n = L - i0
+        q0 = q_ref[i0 : i0 + BLOCK, 0:128]
+        q0 = jnp.where(lane_low(q0.shape), q0, jnp.zeros_like(q0))
+        s = dot(q0, k_ref[i0:L, 0:128], NT) * scale
+        rows = i0 + lax.broadcasted_iota(jnp.int32, (BLOCK, n), 0)
+        cols = i0 + lax.broadcasted_iota(jnp.int32, (BLOCK, n), 1)
+        same = seg_column(segr_ref, i0) == segr_ref[0:1, i0:L]
+        picked = same & (cols > rows) & (startr_ref[0:1, i0:L] == 0)
+        sel = jnp.where(picked, jnp.maximum(s, 0.0), 0.0)
+        if b == nb - 1:
+            below = jnp.zeros((1, n), F32)
+        else:
+            below = jnp.concatenate([jnp.zeros((1, BLOCK), F32), carry], axis=1)
+        carried = split_sum(upper, sel) + below
+        pen_ref[i0 : i0 + BLOCK, i0:L] = jnp.where(same & (cols >= rows), carried * (8.0 / L * LOG2E), BIG)
+        carry = below + jnp.sum(sel, axis=0, keepdims=True)
+    c = scale * LOG2E
     for b in range(nb):
-        i0=b*BLOCK; n=L-i0
-        def pair(p,stats,i0=i0,n=n):
-            off=pl.multiple_of(p*128,128)
-            q=q_ref[i0:i0+BLOCK,pl.ds(off,128)]
-            k=k_ref[i0:L,pl.ds(off,128)]
-            v=v_ref[i0:L,pl.ds(off,128)]
-            low=lane_low(q.shape)
-            outs=[]
-            lane=lax.broadcasted_iota(jnp.int32,(BLOCK,128),1)
+        i0 = b * BLOCK
+        n = L - i0
+
+        def pair(p, stats, i0=i0, n=n):
+            off = pl.multiple_of(p * 128, 128)
+            q = q_ref[i0 : i0 + BLOCK, pl.ds(off, 128)]
+            k = k_ref[i0:L, pl.ds(off, 128)]
+            v = v_ref[i0:L, pl.ds(off, 128)]
+            low = lane_low(q.shape)
+            lowv = lane_low(v.shape)
+            lane = lax.broadcasted_iota(jnp.int32, (BLOCK, 128), 1)
+            outs = []
             for h in range(2):
-                mine=low if h==0 else jnp.logical_not(low)
-                qm=jnp.where(mine,q,jnp.zeros_like(q))
-                s=dot(qm,k,NT)*c-pen_ref[i0:i0+BLOCK,i0:L]
-                m=jnp.max(s,axis=1,keepdims=True)
-                e=jnp.exp2(s-m).astype(BF)
-                lowv=lane_low(v.shape)
-                vm=jnp.where(lowv if h==0 else jnp.logical_not(lowv),v,jnp.ones_like(v))
-                o=dot(e,vm)
-                tot=pltpu.roll(o,HDIM,1)
-                outs.append(o/tot)
-                full=jnp.where(mine,tot,o)
-                stats=jnp.where(lane==2*p+h,m+jnp.log2(full),stats)
-            o_ref[i0:i0+BLOCK,pl.ds(off,128)]=jnp.where(low,outs[0],outs[1]).astype(BF)
+                mine = low if h == 0 else jnp.logical_not(low)
+                s = dot(jnp.where(mine, q, jnp.zeros_like(q)), k, NT) * c - pen_ref[i0 : i0 + BLOCK, i0:L]
+                m = jnp.max(s, axis=1, keepdims=True)
+                e = jnp.exp2(s - m).astype(BF)
+                ones = jnp.where(lowv if h == 0 else jnp.logical_not(lowv), v, jnp.ones_like(v))
+                o = dot(e, ones)
+                total = pltpu.roll(o, HDIM, 1)
+                outs.append(o / total)
+                stats = jnp.where(lane == 2 * p + h, m + jnp.log2(jnp.where(mine, total, o)), stats)
+            o_ref[i0 : i0 + BLOCK, pl.ds(off, 128)] = jnp.where(low, outs[0], outs[1]).astype(BF)
             return stats
-        lse_ref[i0:i0+BLOCK,:]=lax.fori_loop(0,pairs,pair,jnp.zeros((BLOCK,128),F32))
-
-def attn_fwd(q,k,v,seg):
-    L,D=q.shape
-    start=jnp.concatenate([(seg[:-1]!=seg[1:]).astype(jnp.int32),jnp.ones((1,),jnp.int32)])
-    vm=pl.BlockSpec(memory_space=pltpu.VMEM)
-    return pl.pallas_call(attn_fwd_kernel,
-        out_shape=(jax.ShapeDtypeStruct((L,D),BF),jax.ShapeDtypeStruct((L,128),F32),jax.ShapeDtypeStruct((L,L),F32)),
-        in_specs=[vm]*6,out_specs=(vm,)*3,
-        compiler_params=pltpu.CompilerParams(vmem_limit_bytes=60*2**20),name="attn_fwd")(q,k,v,seg[:,None],seg[None,:],start[None,:])
+
+        lse_ref[i0 : i0 + BLOCK, :] = lax.fori_loop(0, HEADS // 2, pair, jnp.zeros((BLOCK, 128), F32))
+
+
+def seg_rows(seg):
+    starts = jnp.concatenate([(seg[:-1] != seg[1:]).astype(jnp.int32), jnp.ones((1,), jnp.int32)])
+    return jnp.stack([seg, starts])
+
+
+def attn_fwd(q, k, v, seg):
+    L, D = q.shape
+    vm = pl.BlockSpec(memory_space=pltpu.VMEM)
+    return pl.pallas_call(
+        attend,
+        out_shape=(
+            jax.ShapeDtypeStruct((L, D), BF), jax.ShapeDtypeStruct((L, 128), F32), jax.ShapeDtypeStruct((L, L), F32)),
+        in_specs=[vm] * 4,
+        out_specs=(vm,) * 3,
+        compiler_params=pltpu.CompilerParams(vmem_limit_bytes=VMEM_LIMIT),
+        name="attn_fwd",
+    )(q, k, v, seg_rows(seg))
+
 
 def attn_bwd_kernel(q_ref,k_ref,v_ref,g_ref,o_ref,lse_ref,pen_ref,startr_ref,out_ref,qt,gt,dkt,dvt,dsum):
     L,D=q_ref.shape; nb=L//BLOCK
@@ -203,7 +227,17 @@
 def layer(tokens, segs, cotangent, weights, fused):
     (w_qkv, q_bias, v_bias, w_out, out_bias, attn_gain, attn_shift, mlp_gain, mlp_shift,
      w_up, up_bias, w_down, down_bias) = weights
-    width = tokens.shape[1]
+    width = tokens.shape[-1]
+    if fused:
+        vectors = jnp.concatenate([q_bias, v_bias, out_bias, attn_gain, attn_shift, mlp_gain, mlp_shift, down_bias, up_bias])
+        vectors = vectors.reshape(-1, width)
+        rows = seg_rows(segs)
+        tokens, cotangent, queries, keys, values, attended, stats, penalty = front(tokens, cotangent, w_qkv, vectors, rows)
+        output, grad_attended, grad_residual, delta, g_w_out, g_w_up, g_w_down, small = middle(
+            attended, tokens, cotangent, vectors, w_out, w_up, w_down)
+        return (output, *attn_back_and_sums(
+            queries, keys, values, grad_attended, delta, stats, rows, tokens, vectors, w_qkv, small,
+            penalty, grad_residual, g_w_out, g_w_down, g_w_up))
     inputs = tokens.astype(F32)
     normal_one, scale_one = norm_parts(inputs)
     normed = (normal_one * attn_gain + attn_shift).astype(BF)
@@ -233,16 +267,6 @@
     g_out_bias = jnp.sum(grad_branch.astype(F32), axis=0)
     g_w_out = dot(attended, grad_branch, ((0,), (0,)))
     grad_attended = dot(grad_branch, w_out, ((1,), (1,))).astype(BF)
-    if fused:
-        grad_attended = lax.optimization_barrier(grad_attended)
-        start_sums = jnp.sum((grad_attended.astype(F32) * attended.astype(F32)).reshape(-1, HEADS, HDIM), axis=2)
-        delta = jnp.pad(start_sums, ((0, 0), (0, 128 - HEADS)))
-        zero = jnp.zeros((width,), F32)
-        small = jnp.concatenate([zero, zero, g_out_bias, zero, zero, g_mlp_gain, g_mlp_shift, g_down_bias, g_up_bias])
-        small = jnp.pad(small.reshape(-1, width), ((0, 4), (0, 0)))
-        return attn_back_and_sums(
-            queries, keys, values, grad_attended, delta, stats, segs, tokens, attn_gain, attn_shift, w_qkv, small,
-            penalty, grad_residual, g_w_out.astype(BF), g_w_down.astype(BF), g_w_up.astype(BF), output)
     grad_proj = attn_bwd(queries, keys, values, grad_attended, attended, stats, penalty, segs)
     bias_sums = jnp.sum(grad_proj.astype(F32), axis=0)
     g_q_bias = bias_sums[:width]
@@ -465,9 +489,9 @@
         self.own.wait()
 
 
-def back_kernel(q_ref, k_ref, v_ref, g_ref, delta_ref, lse_ref, startr_ref, tokens_ref, gain_ref, shift_ref,
-                w_ref, small_ref, pen_ref, residual_ref, g_out_ref, down_ref, up_ref, output_ref,
-                down_out, up_out, side_out, tokens_out, output_out, small_out,
+def back_kernel(q_ref, k_ref, v_ref, g_ref, delta_ref, lse_ref, seg_ref, tokens_ref, vec_ref,
+                w_ref, small_ref, pen_ref, residual_ref, g_out_ref, down_ref, up_ref,
+                down_out, up_out, side_out, tokens_out, small_out,
                 qt, gt, dkt, dvt, dsum, pen, dqkv, side, gtok, gres, own, from_core, from_one, from_two, from_z,
                 sm_acc, sm_rec, sent, landed, local, home_s, home_r, home_l, sm_s, sm_r, pen_s, res_s, out_s):
     L, D = q_ref.shape
@@ -477,6 +501,8 @@
     pairs = HEADS // 2
     width = PANEL // SPLIT
     place = Place()
+    vec = lambda row: vec_ref[row : row + 1, :]
+    startr_ref = seg_ref.at[1:2]
     place.greet(place.along_cols + place.along_z)
     buffers, sems = (own, from_core, from_one, from_two, from_z), (sent, landed, local)
     chunks = []
@@ -494,9 +520,6 @@
     pen_copies = [pltpu.make_async_copy(pen_ref.at[b * BLOCK : (b + 1) * BLOCK, :], pen.at[b % 2], pen_s.at[b % 2]) for b in range(nb)]
     res_copies = [pltpu.make_async_copy(residual_ref.at[b * BLOCK : (b + 1) * BLOCK, :], gres.at[b % 2], res_s.at[b % 2]) for b in range(nb)]
     pen_copies[0].start()
-    output_home = Homeward(place, output_ref, output_out, home_s.at[0], home_r.at[0], home_l.at[0])
-    output_home.start()
-    line.occupy("plane", 16.0)
     out_copy = pltpu.make_async_copy(g_out_ref, side.at[:, 3 * D : 4 * D], out_s)
     out_copy.start()
     for p in range(pairs):
@@ -581,7 +604,7 @@
 
     for b in range(nb):
         normal, _ = normal_of(b)
-        normed = (normal * gain_ref[...] + shift_ref[...]).astype(BF)
+        normed = (normal * vec(ROW_GAIN1) + vec(ROW_SHIFT1)).astype(BF)
         for p in range(pairs):
             qt[p * 128 : (p + 1) * 128, b * BLOCK : (b + 1) * BLOCK] = normed[:, p * 128 : (p + 1) * 128].T
     line.worked(3.0)
@@ -607,11 +630,11 @@
         grad = dot(dqkv[rowsl, :], w_ref[...], NT)
         g_gain = g_gain + jnp.sum(grad * normal, axis=0, keepdims=True)
         g_shift = g_shift + jnp.sum(grad, axis=0, keepdims=True)
-        back = norm_back(grad, normal, spread, gain_ref[...])
+        back = norm_back(grad, normal, spread, vec(ROW_GAIN1))
         res_copies[b].wait()
         gtok[rowsl, :] = (gres[b % 2] + back).astype(BF)
         line.worked(3.0)
-    tokens_home = Homeward(place, gtok, tokens_out, home_s.at[1], home_r.at[1], home_l.at[1])
+    tokens_home = Homeward(place, gtok, tokens_out, home_s, home_r, home_l)
     tokens_home.start()
     line.occupy("plane", 16.0)
     sm_acc[0, 3:4, :] = g_gain
@@ -632,13 +655,11 @@
     line.finish()
     for copy in smalls:
         copy.wait_send()
-    output_home.wait()
     tokens_home.wait()
 
 
-def attn_back_and_sums(q, k, v, g, delta, lse, seg, tokens, gain, shift, w_qkv, small, pen, residual, g_out, down, up, output):
+def attn_back_and_sums(q, k, v, g, delta, lse, segs, tokens, vectors, w_qkv, small, pen, residual, g_out, down, up):
     L, D = q.shape
-    start = jnp.concatenate([(seg[:-1] != seg[1:]).astype(jnp.int32), jnp.ones((1,), jnp.int32)])
     N, W = 3 * SPLIT, PANEL // SPLIT
     hbm = pl.BlockSpec(memory_space=pl.ANY)
     vm = pl.BlockSpec(memory_space=pltpu.VMEM)
@@ -647,9 +668,9 @@
     return pl.pallas_call(
         back_kernel,
         out_shape=(shape(down.shape, BF), shape(up.shape, BF), shape((D, 4 * D), BF),
-                   shape((8, L // 8, D), BF), shape((8, L // 8, D), BF), shape(small.shape, F32)),
-        in_specs=[vm] * 12 + [hbm] * 6,
-        out_specs=(hbm,) * 5 + (vm,),
+                   shape((8, L // 8, D), BF), shape(small.shape, F32)),
+        in_specs=[vm] * 11 + [hbm] * 5,
+        out_specs=(hbm,) * 4 + (vm,),
         scratch_shapes=[
             pltpu.VMEM((D, L), BF), pltpu.VMEM((D, L), BF), pltpu.VMEM((D, L), F32), pltpu.VMEM((D, L), F32),
             pltpu.VMEM((BLOCK, L), F32), pltpu.VMEM((2, BLOCK, L), F32), pltpu.VMEM((L, 3 * D), BF),
@@ -657,12 +678,198 @@
             pltpu.VMEM((N, 2, PANEL, W), BF), pltpu.VMEM((N, 2, PANEL, W), BF), pltpu.VMEM((N, 2, PANEL // 2, W), BF),
             pltpu.VMEM((N, 2, PANEL // 4, W), BF), pltpu.VMEM((N, 2, 3, PANEL // 16, W), BF),
             pltpu.VMEM((5,) + small.shape, F32), pltpu.VMEM((5,) + small.shape, F32),
-            dma((N, 24)), dma((N, 24)), dma((N, 4)), dma((2, 7)), dma((2, 7)), dma((2,)), dma((5,)), dma((5,)),
+            dma((N, 24)), dma((N, 24)), dma((N, 4)), dma((7,)), dma((7,)), dma, dma((5,)), dma((5,)),
             dma((2,)), dma((2,)), dma,
         ],
         compiler_params=pltpu.CompilerParams(vmem_limit_bytes=VMEM_LIMIT, collective_id=1, has_side_effects=True),
         name="attn_back_and_sums",
-    )(q, k, v, g, delta, lse, start[None, :], tokens, gain[None, :], shift[None, :], w_qkv, small, pen, residual, g_out, down, up, output)
+    )(q, k, v, g, delta, lse, segs, tokens, vectors, w_qkv, small, pen, residual, g_out, down, up)
+
+
+def front_kernel(tokens_ref, cot_ref, w_ref, vec_ref, seg_ref,
+                 tokens_out, cot_out, q_ref, k_ref, v_ref, o_ref, lse_ref, pen_ref,
+                 whole, w, sent, landed, local):
+    L, D = q_ref.shape
+    part = L // 8
+    place = Place()
+    z, y, x, c, col = place.z, place.y, place.x, place.c, place.col
+
+    def other(k):
+        flip = lambda bit, coord: 1 - coord if bit else coord
+        return (z, flip(k & 4, y) * 4 + flip(k & 2, x) * 2 + flip(k & 1, c))
+
+    place.greet([other(k) for k in range(1, 8)])
+    mine = pl.multiple_of(col * part, 16)
+    out = [remote(tokens_ref.at[other(k)[1]], rows_at(whole, mine, part), sent.at[0, k], landed.at[0, k], other(k))
+           for k in range(1, 8)]
+    own = pltpu.make_async_copy(tokens_ref.at[col], rows_at(whole, mine, part), local.at[0])
+    load = pltpu.make_async_copy(w_ref, w, local.at[1])
+    cots = [remote(cot_ref.at[other(k)[1]], rows_at(cot_out, mine, part), sent.at[1, k], landed.at[1, k], other(k))
+            for k in range(1, 8)]
+    cot_own = pltpu.make_async_copy(cot_ref.at[col], rows_at(cot_out, mine, part), local.at[2])
+    keep = pltpu.make_async_copy(whole, tokens_out, local.at[3])
+    own.start()
+    for copy in out:
+        copy.start()
+    load.start()
+    cot_own.start()
+    own.wait()
+    load.wait()
+    vec = lambda row: vec_ref[row : row + 1, :]
+    for chip in range(4):
+        for k in (2 * chip, 2 * chip + 1):
+            if k:
+                out[k - 1].wait_recv()
+        if chip == 3:
+            for copy in cots:
+                copy.start()
+        first = other(2 * chip)[1] - c
+        here = pl.ds(pl.multiple_of(first * part, 16), 2 * part)
+        normal, _ = norm_parts(whole[here, :].astype(F32))
+        normed = (normal * vec(ROW_GAIN1) + vec(ROW_SHIFT1)).astype(BF)
+        q_ref[here, :] = (dot(normed, w[:, 0:D]) + vec(ROW_Q)).astype(BF)
+        k_ref[here, :] = dot(normed, w[:, D : 2 * D]).astype(BF)
+        v_ref[here, :] = (dot(normed, w[:, 2 * D : 3 * D]) + vec(ROW_V)).astype(BF)
+    keep.start()
+    attend(q_ref, k_ref, v_ref, seg_ref, o_ref, lse_ref, pen_ref)
+    keep.wait()
+    cot_own.wait()
+    for copy in out:
+        copy.wait_send()
+    for copy in cots:
+        copy.wait()
+
+
+def front(tokens, cotangent, w_qkv, vectors, segs):
+    cols, part, D = tokens.shape
+    L = cols * part
+    hbm = pl.BlockSpec(memory_space=pl.ANY)
+    vm = pl.BlockSpec(memory_space=pltpu.VMEM)
+    dma = pltpu.SemaphoreType.DMA
+    rows = jax.ShapeDtypeStruct((L, D), BF)
+    return pl.pallas_call(
+        front_kernel,
+        out_shape=(rows,) * 6 + (jax.ShapeDtypeStruct((L, 128), F32), jax.ShapeDtypeStruct((L, L), F32)),
+        in_specs=[hbm] * 3 + [vm] * 2,
+        out_specs=(hbm,) * 2 + (vm,) * 6,
+        scratch_shapes=[pltpu.VMEM((L, D), BF), pltpu.VMEM((D, 3 * D), BF), dma((2, 8)), dma((2, 8)), dma((4,))],
+        compiler_params=pltpu.CompilerParams(vmem_limit_bytes=VMEM_LIMIT, collective_id=2, has_side_effects=True),
+        name="front",
+    )(tokens, cotangent, w_qkv, vectors, segs)
+
+
+ROW_Q, ROW_V, ROW_OUT, ROW_GAIN1, ROW_SHIFT1, ROW_GAIN2, ROW_SHIFT2, ROW_DOWN, ROW_UP = range(9)
+
+
+def gelu_pair(u):
+    slope = 0.7978845608028654
+    square = u * u
+    t = jnp.tanh(slope * u * (1.0 + 0.044715 * square))
+    half = 0.5 * (1.0 + t)
+    return u * half, half + (0.5 * slope) * u * (1.0 - t * t) * (1.0 + 3 * 0.044715 * square)
+
+
+def middle_kernel(att_ref, tok_ref, cot_ref, vec_ref, w_out_ref, w_up_ref, w_down_ref,
+                  output_out, g_ref, res_ref, delta_ref, g_out_ref, g_up_ref, g_down_ref, small_ref,
+                  w_out, w_up, w_down, act, gu, n2t, dyt, gb, out, load, sent, landed, local):
+    L, D = att_ref.shape
+    ff = w_up.shape[1]
+    place = Place()
+    place.greet(place.along_cols)
+    loads = [pltpu.make_async_copy(a, b, load.at[i])
+             for i, (a, b) in enumerate(((w_out_ref, w_out), (w_up_ref, w_up), (w_down_ref, w_down)))]
+    for copy in loads:
+        copy.start()
+    small_ref[...] = jnp.zeros_like(small_ref)
+    features = lax.broadcasted_iota(jnp.int32, (D, 128), 0) // HDIM
+    member = jnp.where(features == lax.broadcasted_iota(jnp.int32, (D, 128), 1), 1.0, 0.0).astype(BF)
+    vec = lambda row: vec_ref[row : row + 1, :]
+
+    def add_row(row, values):
+        small_ref[row : row + 1, :] += jnp.sum(values, axis=0, keepdims=True)
+
+    for copy in loads:
+        copy.wait()
+
+    def block(b, carry):
+        here = pl.ds(pl.multiple_of(b * ROWS, ROWS), ROWS)
+        att = att_ref[here, :]
+        dy = cot_ref[here, :]
+        residual = tok_ref[here, :].astype(F32) + dot(att, w_out[...]) + vec(ROW_OUT)
+        normal, spread = norm_parts(residual)
+        n2 = (normal * vec(ROW_GAIN2) + vec(ROW_SHIFT2)).astype(BF)
+        n2t[:, here] = n2.T
+        dyt[:, here] = dy.T
+        top = dy.astype(F32)
+        add_row(ROW_DOWN, top)
+        total = residual + vec(ROW_DOWN)
+        grad_two = jnp.zeros((ROWS, D), F32)
+        for j in range(ff // D):
+            part = slice(j * D, (j + 1) * D)
+            value, slope = gelu_pair(dot(n2, w_up[:, part]) + vec(ROW_UP + j))
+            low = value.astype(BF)
+            act[here, part] = low
+            total = total + dot(low, w_down[part, :])
+            grad = (dot(dy, w_down[part, :], NT) * slope).astype(BF)
+            gu[here, part] = grad
+            add_row(ROW_UP + j, grad.astype(F32))
+            grad_two = grad_two + dot(grad, w_up[:, part], NT)
+        out[here, :] = total.astype(BF)
+        add_row(ROW_GAIN2, grad_two * normal)
+        add_row(ROW_SHIFT2, grad_two)
+        grad_residual = top + norm_back(grad_two, normal, spread, vec(ROW_GAIN2))
+        res_ref[here, :] = grad_residual
+        branch = grad_residual.astype(BF)
+        gb[here, :] = branch
+        add_row(ROW_OUT, branch.astype(F32))
+        grad_att = dot(branch, w_out[...], NT).astype(BF)
+        g_ref[here, :] = grad_att
+        product = grad_att.astype(F32) * att.astype(F32)
+        high = product.astype(BF)
+        delta_ref[here, :] = dot(high, member) + dot((product - high.astype(F32)).astype(BF), member)
+        return carry
+
+    lax.fori_loop(0, L // ROWS, block, 0)
+    home = Homeward(place, out, output_out, sent, landed, local)
+    home.start()
+
+    def down(i, carry):
+        part = pl.ds(pl.multiple_of(i * 256, 256), 256)
+        g_down_ref[part, :] = dot(dyt[...], act[:, part]).astype(BF).T
+        return carry
+
+    def up(i, carry):
+        part = pl.ds(pl.multiple_of(i * 256, 256), 256)
+        g_up_ref[:, part] = dot(n2t[...], gu[:, part]).astype(BF)
+        return carry
+
+    lax.fori_loop(0, ff // 256, down, 0)
+    lax.fori_loop(0, ff // 256, up, 0)
+    g_out_ref[...] = dot(att_ref[...], gb[...], ((0,), (0,))).astype(BF)
+    home.wait()
+
+
+def middle(attended, tokens, cotangent, vectors, w_out, w_up, w_down):
+    L, D = attended.shape
+    ff = w_up.shape[1]
+    hbm = pl.BlockSpec(memory_space=pl.ANY)
+    vm = pl.BlockSpec(memory_space=pltpu.VMEM)
+    dma = pltpu.SemaphoreType.DMA
+    shape = jax.ShapeDtypeStruct
+    return pl.pallas_call(
+        middle_kernel,
+        out_shape=(shape((8, L // 8, D), BF), shape((L, D), BF), shape((L, D), F32), shape((L, 128), F32),
+                   shape((D, D), BF), shape((D, ff), BF), shape((ff, D), BF), shape((16, D), F32)),
+        in_specs=[vm] * 4 + [hbm] * 3,
+        out_specs=(hbm,) + (vm,) * 7,
+        scratch_shapes=[
+            pltpu.VMEM((D, D), BF), pltpu.VMEM((D, ff), BF), pltpu.VMEM((ff, D), BF), pltpu.VMEM((L, ff), BF),
+            pltpu.VMEM((L, ff), BF), pltpu.VMEM((D, L), BF), pltpu.VMEM((D, L), BF), pltpu.VMEM((L, D), BF),
+            pltpu.VMEM((L, D), BF), dma((3,)), dma((7,)), dma((7,)), dma,
+        ],
+        compiler_params=pltpu.CompilerParams(vmem_limit_bytes=VMEM_LIMIT, collective_id=3, has_side_effects=True),
+        name="middle",
+    )(attended, tokens, cotangent, vectors, w_out, w_up, w_down)
 
 
 def summed_grads(grads, copies):
@@ -681,19 +888,6 @@
     return out
 
 
-def whole_by_permutes(value):
-    parts, cols = value.shape[0], lax.axis_size("cols")
-    me = lax.axis_index("cols")
-    whole = jnp.zeros_like(value)
-    own = lax.dynamic_slice_in_dim(value, me, 1, 0)
-    whole = lax.dynamic_update_slice_in_dim(whole, own, me, 0)
-    for step in range(1, cols):
-        block = lax.dynamic_slice_in_dim(value, lax.rem(me + step, cols), 1, 0)
-        block = lax.ppermute(block, "cols", [(i, (i + step) % cols) for i in range(cols)])
-        whole = lax.dynamic_update_slice_in_dim(whole, block, lax.rem(me - step + cols, cols), 0)
-    return whole
-
-
 def per_device(tokens, segment_ids, cotangent, *weights):
     seqs, part, width = tokens.shape
     cols = lax.axis_size("cols")
@@ -702,17 +896,14 @@
     held = max(1, seqs // cols)
     first = (lax.axis_index("cols") // copies) * held
     segs = lax.dynamic_slice_in_dim(segment_ids, first, held, 0)
+    if fitting:
+        output, down, up, side, grad_tokens, small = layer(tokens, segs[0], cotangent, weights, True)
+        return (
+            output, grad_tokens.astype(F32), side[:, : 3 * width].astype(F32), small[ROW_Q], small[ROW_V],
+            side[:, 3 * width :].astype(F32), small[ROW_OUT], small[ROW_GAIN1], small[ROW_SHIFT1], small[ROW_GAIN2],
+            small[ROW_SHIFT2], up.astype(F32), small[ROW_UP:12].reshape(-1), down.astype(F32), small[ROW_DOWN])
     tokens_whole = to_whole(tokens, copies)
-    if fitting:
-        cotangent_whole = whole_by_permutes(cotangent).reshape(1, -1, width)
-    else:
-        cotangent_whole = to_whole(cotangent, copies)
-    if fitting:
-        down, up, side, grad_tokens, output, small = layer(tokens_whole[0], segs[0], cotangent_whole[0], weights, True)
-        return (
-            output, grad_tokens.astype(F32), side[:, : 3 * width].astype(F32), small[0], small[1],
-            side[:, 3 * width :].astype(F32), small[2], small[3], small[4], small[5], small[6],
-            up.astype(F32), small[8:12].reshape(-1), down.astype(F32), small[7])
+    cotangent_whole = to_whole(cotangent, copies)
     results = [
         layer(tokens_whole[s], segs[s], cotangent_whole[s], weights, False) for s in range(held)
     ]

time: 401 us -> 332 us (0.83)
  matrix products: 82.3 us -> 0 us
  Pallas kernels: 213 us -> 292 us
  waiting for transfers between devices: 22.1 us -> 0 us
  other arithmetic: 40.7 us -> 20.4 us
  local copies, waits for them, and re-layouts: 23.8 us -> 12.3 us
  starting transfers between devices: 10.7 us -> 0 us
    pallas_call x1 -> x2, Pallas kernels: 31 us -> 118 us  [the longest x1 63.2 us: middle(): pl.pallas_call(middle_kernel, out_shape=(shape((8, L // 8, D), BF), shape...]
    dot_general x10 -> x0, matrix products: 82.3 us -> none  [dot(): return lax.dot_general(a, b, (dims, ((), ())), preferred_element_type=F32)]
    ppermute x7 -> x0, waiting for transfers between devices: 22.1 us -> none  [whole_by_permutes(): lax.ppermute(block, 'cols', [(i, (i + step) % cols) for i in range(cols)])]
    reduce_sum x6 -> x0, other arithmetic: 10.7 us -> none  [the longest x1 2.58 us: layer(): g_out_bias = jnp.sum(grad_branch.astype(F32), axis=0)]
    pallas_call x1, Pallas kernels: 182 us -> 174 us  [attn_back_and_sums(): pl.pallas_call(back_kernel, out_shape=(shape(down.shape, BF), shape(up.sh...]
    all_to_all x1 -> x0, starting transfers between devices: 5.45 us -> none  [to_whole(): return lax.all_to_all(value, 'cols', 0, 1, tiled=True)]
    ppermute x7 -> x0, starting transfers between devices: 5.25 us -> none  [whole_by_permutes(): lax.ppermute(block, 'cols', [(i, (i + step) % cols) for i in range(cols)])]
    dynamic_update_slice x7 -> x0, local copies, waits for them, and re-layouts: 4.83 us -> none  [whole_by_permutes(): lax.dynamic_update_slice_in_dim(whole, block, lax.rem(me - step + cols, c...]
  transfers between devices with their start and end apart: 8 -> 0, of which waited for: 2 -> 0; matrix products, arithmetic and copies ran while one was open for 4% -> 0% of each run, Pallas kernels for 0% -> 0%
where the time goes in v1:
time: 332 us; the launch traced here: 326 us
  Pallas kernels  292 us (88%)
  other arithmetic  20.4 us (6%)
  local copies, waits for them, and re-layouts  12.3 us (4%)
    pallas_call x1, Pallas kernels, attn_back_and_sums(): pl.pallas_call(back_kernel, out_shape=(shape(down.shape, BF), shape(up.sh...  174 us
    pallas_call x1, Pallas kernels, middle(): pl.pallas_call(middle_kernel, out_shape=(shape((8, L // 8, D), BF), shape...  63.2 us
    pallas_call x1, Pallas kernels, front(): pl.pallas_call(front_kernel, out_shape=(rows,) * 6 + (jax.ShapeDtypeStruc...  54.3 us
    unnamed x19, local copies, waits for them, and re-layouts  6.99 us

profile of v1, /device:TPU:0, one launch (start us, length us, event | category | flops | bytes accessed | tf_op | source)
XLA Modules:
  0.0 325.8 jit_solution(5350204294162354409)
XLA Ops:
  0.7 0.9 compare_reduce_fusion
  1.6 0.1 add_convert_fusion
  1.7 0.8 constant_dynamic-slice_fusion
  2.4 0.6 pad_add_fusion.seg_ref
  3.0 0.7 constant_dynamic-update-slice_fusion.8
  3.7 0.7 constant_dynamic-update-slice_fusion.7
  4.4 0.7 constant_dynamic-update-slice_fusion.6
  5.1 0.7 constant_dynamic-update-slice_fusion.5
  5.8 0.7 constant_dynamic-update-slice_fusion.4
  6.5 0.7 constant_dynamic-update-slice_fusion.3
  7.2 0.7 constant_dynamic-update-slice_fusion.2
  7.9 0.7 constant_dynamic-update-slice_fusion.1
  8.6 0.7 constant_dynamic-update-slice_fusion
  9.3 0.6 reshape.41.vec_ref
  9.9 54.3 %front.1 = (bf16[1024,768]{1,0:T(8,128)(2,1)}, bf16[1024,768]{1,0:T(8,128)(2,1)}, bf16[1024,768]{1,0:T(8,128)(2,1)}, bf16[1024,768]{1,0:T(8,128)(2,1)}, bf16[102...) custom-call(bf16[8,128,768]{2,1,0:T(8,128)(2,1)} %tokens_ref.1, ...), custom_call_target="tpu_custom_call" | custom-call | tf_op jit(solution)/shard_map/front/pallas_call | solution.py:750
  64.2 63.2 %middle.1 = (bf16[8,128,768]{2,1,0:T(8,128)(2,1)}, bf16[1024,768]{1,0:T(8,128)(2,1)}, f32[1024,768]{1,0:T(8,128)}, f32[1024,128]{1,0:T(8,128)}, bf16[768,768]{1,...) custom-call(bf16[1024,768]{1,0:T(8,128)(2,1)} %get-tuple-element.36.att_ref, ...), custom_call_target="tpu_custom_call" | custom-call | tf_op jit(solution)/shard_map/middle/pallas_call | solution.py:859
  127.5 174.5 %attn_back_and_sums.1 = (bf16[3072,768]{1,0:T(8,128)(2,1)}, bf16[768,3072]{1,0:T(8,128)(2,1)}, bf16[768,3072]{1,0:T(8,128)(2,1)}, bf16[8,128,768]{2,1,0:T(8,128)(2,1)}, f32[16,768]{1,0:T(8,128)}) custom-call(bf16[1024,768]{1,0:T(8,128)(2,1)} %get-tuple-element.40.q_ref, bf16[1024,768]{1,0:T(8,128)(2,1)} %get-tuple-element.41.k_ref, ...), custom_call_target="tpu_custom_call" | custom-call | tf_op jit(solution)/shard_map/attn_back_and_sums/pallas_call | solution.py:668
  302.0 0.7 slice.52
  302.7 1.9 slice_reduce_fusion
  304.5 0.6 reshape.42
  305.2 0.0 copy-start.1
  305.2 3.5 %convert_element_type.20 = f32[8,128,768]{2,1,0:T(8,128)} convert(bf16[8,128,768]{2,1,0:T(8,128)(2,1)} %get-tuple-element.52) | non-fusion elementwise | flops 786432 | bytes 4718592 | tf_op jit(solution)/shard_map/convert_element_type | solution.py:902
  308.7 0.0 copy-done.1
  308.7 1.6 slice_convert_fusion.1
  310.2 0.0 copy-start
  310.2 0.0 slice-start
  310.3 4.2 %slice_convert_fusion = f32[768,2304]{1,0:T(8,128)} fusion(bf16[768,3072]{1,0:T(8,128)(2,1)S(1)} %copy-done.1), kind=kLoop, calls=%fused_computation | loop fusion | flops 1769472 | bytes 10616832 | tf_op jit(solution)/shard_map/convert_element_type | solution.py:902
  314.4 0.3 copy-done
  314.7 0.0 slice-start.1
  314.7 5.0 %convert_element_type.23 = f32[768,3072]{1,0:T(8,128)} convert(bf16[768,3072]{1,0:T(8,128)(2,1)S(1)} %copy-done) | non-fusion elementwise | flops 2359296 | bytes 14155776 | tf_op jit(solution)/shard_map/convert_element_type | solution.py:904
  319.7 0.0 slice-done
  319.7 0.0 slice-done.1
  319.7 0.0 copy-start.2
  319.8 4.5 %convert_element_type.24 = f32[3072,768]{1,0:T(8,128)} convert(bf16[3072,768]{1,0:T(8,128)(2,1)S(1)} %bitcast.2) | non-fusion elementwise | flops 2359296 | bytes 14155776 | tf_op jit(solution)/shard_map/convert_element_type | solution.py:904
  324.2 0.0 copy-done.2
  324.2 1.1 copy.41
  (2 shorter events, 0.0 us)
Async XLA Ops:
  305.2 3.5 %copy-start.1 = (bf16[768,3072]{1,0:T(8,128)(2,1)S(1)}, bf16[768,3072]{1,0:T(8,128)(2,1)}, u32[]{:S(2)}) copy-start(bf16[768,3072]{1,0:T(8,128)(2,1)} %get-tuple-element.53) | copy-start | bytes 14155780
  310.2 4.4 %copy-start = (bf16[768,3072]{1,0:T(8,128)(2,1)S(1)}, bf16[768,3072]{1,0:T(8,128)(2,1)}, u32[]{:S(2)}) copy-start(bf16[768,3072]{1,0:T(8,128)(2,1)} %get-tuple-element.55) | copy-start | bytes 14155780
  310.2 9.5 %slice-start = ((s8[4718592]{0:T(1024)(128)(4,1)}), s8[4194304]{0:T(1024)(128)(4,1)S(1)}, s32[]{:S(2)}) async-start(s8[4718592]{0:T(1024)(128)(4,1)} %bitcast.1), calls=%async_computation | async-start | bytes 8388608
  314.7 5.1 %slice-start.1 = ((s8[4718592]{0:T(1024)(128)(4,1)}), s8[524288]{0:T(1024)(128)(4,1)S(1)}, s32[]{:S(2)}) async-start(s8[4718592]{0:T(1024)(128)(4,1)} %bitcast.1), calls=%async_computation.1 | async-start | bytes 1048576
  319.7 4.5 %copy-start.2 = (bf16[8,128,768]{2,1,0:T(8,128)(2,1)S(1)}, bf16[8,128,768]{2,1,0:T(8,128)(2,1)}, u32[]{:S(2)}) copy-start(bf16[8,128,768]{2,1,0:T(8,128)(2,1)} %get-tuple-element.80) | copy-start | bytes 4718596

commit v2 on v1

--- a/solution.py
+++ b/solution.py
@@ -16,7 +16,9 @@
 BLOCK = 256
 MESH = pl.DeviceIdType.MESH
 PANEL = 768
-SPLIT = 2
+SPLIT = 3
+SLOTS = 2 * SPLIT
+LAG = 1.0
 STEP = 48
 ROWS = 256
 VMEM_LIMIT = 62 * 2**20
@@ -233,11 +235,9 @@
         vectors = vectors.reshape(-1, width)
         rows = seg_rows(segs)
         tokens, cotangent, queries, keys, values, attended, stats, penalty = front(tokens, cotangent, w_qkv, vectors, rows)
-        output, grad_attended, grad_residual, delta, g_w_out, g_w_up, g_w_down, small = middle(
-            attended, tokens, cotangent, vectors, w_out, w_up, w_down)
-        return (output, *attn_back_and_sums(
-            queries, keys, values, grad_attended, delta, stats, rows, tokens, vectors, w_qkv, small,
-            penalty, grad_residual, g_w_out, g_w_down, g_w_up))
+        output, grad_tokens, down, up, side, small = rest(
+            attended, tokens, cotangent, queries, keys, values, stats, penalty, vectors, rows, w_qkv, w_out, w_up, w_down)[:6]
+        return output, down, up, side, grad_tokens, small
     inputs = tokens.astype(F32)
     normal_one, scale_one = norm_parts(inputs)
     normed = (normal_one * attn_gain + attn_shift).astype(BF)
@@ -331,7 +331,7 @@
 
 class Chunk:
     def __init__(self, place, n, source, result, tall, first, buffers, sems):
-        own, from_core, from_one, from_two, from_z = [b.at[n] for b in buffers]
+        own, from_core, from_one, from_two, from_z = [b.at[n % SLOTS] for b in buffers]
         sent, landed, local = sems
         width = own.shape[-1]
         x, y, z, c = place.x, place.y, place.z, place.c
@@ -427,8 +427,8 @@
 
 class Timeline:
     LINK = ["core", "plane", "plane", "deep", "deep", "plane", "plane", "core"]
-    TAKES = [2.5, 6.0, 3.0, 6.0, 6.0, 3.0, 6.0, 2.5]
-    WORK = [2.0, 1.0, 0.5, 0.5, 0.1, 0.1, 0.1, 0.1]
+    TAKES = [t * LAG * 2 / SPLIT for t in (2.5, 6.3, 3.2, 5.8, 5.8, 3.2, 6.3, 2.5)]
+    WORK = [t * 2 / SPLIT for t in (2.0, 1.0, 0.5, 0.5, 0.1, 0.1, 0.1, 0.1)]
 
     def __init__(self):
         self.now = 0.0
@@ -438,12 +438,15 @@
 
     def occupy(self, link, takes):
         self.free[link] = max(self.free[link], self.now) + takes
-        return self.free[link] + 1.5
+        return self.free[link] + 2.0
 
     def begin(self, chunk, then=None):
         chunk.begin()
         self.moving[chunk] = (self.occupy(self.LINK[0], self.TAKES[0]), 0)
         self.after_first[chunk] = then
+
+    def begin_all(self, chunks):
+        self.begin(chunks[0], (lambda: self.begin_all(chunks[1:])) if chunks[1:] else None)
 
     def turn(self, chunk):
         done, k = self.moving.pop(chunk)
@@ -466,6 +469,10 @@
         self.now += takes
         self.ready()
 
+    def complete(self, chunk):
+        while chunk in self.moving:
+            self.turn(min(self.moving, key=lambda c: self.moving[c][0]))
+
     def finish(self):
         while self.moving:
             self.turn(min(self.moving, key=lambda c: self.moving[c][0]))
@@ -487,203 +494,6 @@
         for copy in self.copies:
             copy.wait()
         self.own.wait()
-
-
-def back_kernel(q_ref, k_ref, v_ref, g_ref, delta_ref, lse_ref, seg_ref, tokens_ref, vec_ref,
-                w_ref, small_ref, pen_ref, residual_ref, g_out_ref, down_ref, up_ref,
-                down_out, up_out, side_out, tokens_out, small_out,
-                qt, gt, dkt, dvt, dsum, pen, dqkv, side, gtok, gres, own, from_core, from_one, from_two, from_z,
-                sm_acc, sm_rec, sent, landed, local, home_s, home_r, home_l, sm_s, sm_r, pen_s, res_s, out_s):
-    L, D = q_ref.shape
-    nb = L // BLOCK
-    scale = HDIM**-0.5
-    c = scale * LOG2E
-    pairs = HEADS // 2
-    width = PANEL // SPLIT
-    place = Place()
-    vec = lambda row: vec_ref[row : row + 1, :]
-    startr_ref = seg_ref.at[1:2]
-    place.greet(place.along_cols + place.along_z)
-    buffers, sems = (own, from_core, from_one, from_two, from_z), (sent, landed, local)
-    chunks = []
-    for source, result, tall in ((down_ref, down_out, True), (up_ref, up_out, False), (side, side_out, False)):
-        for j in range(SPLIT):
-            chunks.append(Chunk(place, len(chunks), source, result, tall, j * width, buffers, sems))
-    early = 2 * SPLIT
-    line = Timeline()
-
-    def chain(n):
-        if n < early:
-            line.begin(chunks[n], lambda: chain(n + 1))
-
-    chain(0)
-    pen_copies = [pltpu.make_async_copy(pen_ref.at[b * BLOCK : (b + 1) * BLOCK, :], pen.at[b % 2], pen_s.at[b % 2]) for b in range(nb)]
-    res_copies = [pltpu.make_async_copy(residual_ref.at[b * BLOCK : (b + 1) * BLOCK, :], gres.at[b % 2], res_s.at[b % 2]) for b in range(nb)]
-    pen_copies[0].start()
-    out_copy = pltpu.make_async_copy(g_out_ref, side.at[:, 3 * D : 4 * D], out_s)
-    out_copy.start()
-    for p in range(pairs):
-        qt[p * 128 : (p + 1) * 128, :] = q_ref[:, p * 128 : (p + 1) * 128].T
-        gt[p * 128 : (p + 1) * 128, :] = g_ref[:, p * 128 : (p + 1) * 128].T
-    dkt[...] = jnp.zeros_like(dkt)
-    dvt[...] = jnp.zeros_like(dvt)
-    line.worked(2.0)
-    lower = tri(BLOCK, False)
-    carry = jnp.zeros((1, L), F32)
-    for b in range(nb):
-        i0 = b * BLOCK
-        n = L - i0
-        rowsl = slice(i0, i0 + BLOCK)
-        carry = carry[:, -n:]
-        pen_copies[b].wait()
-        if b + 1 < nb:
-            pen_copies[b + 1].start()
-        pen_b = pen.at[b % 2, :, i0:L]
-
-        def head(p, h):
-            off = p * 128 if isinstance(p, int) else pl.multiple_of(p * 128, 128)
-            q = q_ref[rowsl, pl.ds(off, 128)]
-            g = g_ref[rowsl, pl.ds(off, 128)]
-            k = k_ref[i0:L, pl.ds(off, 128)]
-            v = v_ref[i0:L, pl.ds(off, 128)]
-            low = lane_low(q.shape)
-            mine = low if h == 0 else jnp.logical_not(low)
-            lane = lax.broadcasted_iota(jnp.int32, (BLOCK, 128), 1)
-            lse = jnp.sum(jnp.where(lane == 2 * p + h, lse_ref[rowsl, :], 0.0), axis=1, keepdims=True)
-            delta = jnp.sum(jnp.where(lane == 2 * p + h, delta_ref[rowsl, :], 0.0), axis=1, keepdims=True)
-            s = dot(jnp.where(mine, q, jnp.zeros_like(q)), k, NT)
-            pr = jnp.exp2(s * c - pen_b[...] - lse)
-            dp = dot(jnp.where(mine, g, jnp.zeros_like(g)), v, NT)
-            return s, pr, pr * (dp - delta), off, k
-
-        def finish(p, h, pr, ds, k):
-            base = p * 128 + h * HDIM
-            if not isinstance(p, int):
-                base = pl.multiple_of(base, 64)
-            dsb = ds.astype(BF)
-            dvt[pl.ds(base, HDIM), i0:L] += dot(gt[pl.ds(base, HDIM), rowsl], pr.astype(BF))
-            dkt[pl.ds(base, HDIM), i0:L] += dot(qt[pl.ds(base, HDIM), rowsl], dsb)
-            return dot(dsb, k)
-
-        def pair(p, carry_):
-            dq = []
-            for h in range(2):
-                s, pr, ds, off, k = head(p, h)
-                dsum[:, i0:L] += ds
-                dq.append(finish(p, h, pr, ds, k))
-            dqkv[rowsl, pl.ds(off, 128)] = (jnp.where(lane_low(dq[0].shape), dq[0], dq[1]) * scale).astype(BF)
-            return carry_
-
-        dsum[:, i0:L] = jnp.zeros((BLOCK, n), F32)
-        each = 0.62 * (nb - b)
-        for begin, end in ((1, 3), (3, pairs)) if b < 2 else ((1, pairs),):
-            lax.fori_loop(begin, end, pair, 0)
-            line.worked(each * (end - begin))
-        s, pr, ds, off, k = head(0, 1)
-        dsum[:, i0:L] += ds
-        dq1 = finish(0, 1, pr, ds, k)
-        s, pr, ds, off, k = head(0, 0)
-        total = dsum[:, i0:L] + ds
-        rows = i0 + lax.broadcasted_iota(jnp.int32, (BLOCK, n), 0)
-        cols = i0 + lax.broadcasted_iota(jnp.int32, (BLOCK, n), 1)
-        picked = (pen_b[...] < 1e29) & (cols > rows) & (startr_ref[0:1, i0:L] == 0) & (s > 0)
-        gsel = (split_sum(lower, total) + carry) * (-8.0 / L)
-        carry = carry + jnp.sum(total, axis=0, keepdims=True)
-        ds = ds + jnp.where(picked, gsel, 0.0)
-        dq0 = finish(0, 0, pr, ds, k)
-        dqkv[rowsl, 0:128] = (jnp.where(lane_low(dq0.shape), dq0, dq1) * scale).astype(BF)
-        line.worked(each * 1.2)
-    for p in range(pairs):
-        sl = slice(p * 128, (p + 1) * 128)
-        dqkv[:, D + p * 128 : D + (p + 1) * 128] = (dkt[sl, :] * scale).T.astype(BF)
-        dqkv[:, 2 * D + p * 128 : 2 * D + (p + 1) * 128] = dvt[sl, :].T.astype(BF)
-
-    def normal_of(b):
-        values = tokens_ref[b * BLOCK : (b + 1) * BLOCK, :].astype(F32)
-        return norm_parts(values)
-
-    for b in range(nb):
-        normal, _ = normal_of(b)
-        normed = (normal * vec(ROW_GAIN1) + vec(ROW_SHIFT1)).astype(BF)
-        for p in range(pairs):
-            qt[p * 128 : (p + 1) * 128, b * BLOCK : (b + 1) * BLOCK] = normed[:, p * 128 : (p + 1) * 128].T
-    line.worked(3.0)
-    out_copy.wait()
-    for j in range(SPLIT):
-        for panel in range(3):
-            at = slice(panel * D + j * width, panel * D + (j + 1) * width)
-            side[:, at] = dot(qt[...], dqkv[:, at]).astype(BF)
-        line.now += 2.5
-        line.begin(chunks[early + j])
-        line.ready()
-    sm_acc[0] = small_ref[...]
-    sm_acc[0, 0:1, :] = jnp.sum(dqkv[:, 0:D].astype(F32), axis=0, keepdims=True)
-    sm_acc[0, 1:2, :] = jnp.sum(dqkv[:, 2 * D : 3 * D].astype(F32), axis=0, keepdims=True)
-    res_copies[0].start()
-    g_gain = jnp.zeros((1, D), F32)
-    g_shift = jnp.zeros((1, D), F32)
-    for b in range(nb):
-        rowsl = slice(b * BLOCK, (b + 1) * BLOCK)
-        if b + 1 < nb:
-            res_copies[b + 1].start()
-        normal, spread = normal_of(b)
-        grad = dot(dqkv[rowsl, :], w_ref[...], NT)
-        g_gain = g_gain + jnp.sum(grad * normal, axis=0, keepdims=True)
-        g_shift = g_shift + jnp.sum(grad, axis=0, keepdims=True)
-        back = norm_back(grad, normal, spread, vec(ROW_GAIN1))
-        res_copies[b].wait()
-        gtok[rowsl, :] = (gres[b % 2] + back).astype(BF)
-        line.worked(3.0)
-    tokens_home = Homeward(place, gtok, tokens_out, home_s, home_r, home_l)
-    tokens_home.start()
-    line.occupy("plane", 16.0)
-    sm_acc[0, 3:4, :] = g_gain
-    sm_acc[0, 4:5, :] = g_shift
-    z, col = place.z, place.col
-    friends = [place.core, place.across_x, place.across_y, (z + 1 - 2 * (z % 2), col), (lax.rem(z + 2, 4), col)]
-    smalls = [remote(sm_acc.at[i], sm_rec.at[i], sm_s.at[i], sm_r.at[i], friends[i]) for i in range(5)]
-    smalls[0].start()
-    for i in range(5):
-        line.worked(4.0)
-        smalls[i].wait_recv()
-        following = sm_acc[i] + sm_rec[i]
-        if i < 4:
-            sm_acc[i + 1] = following
-            smalls[i + 1].start()
-        else:
-            small_out[...] = following
-    line.finish()
-    for copy in smalls:
-        copy.wait_send()
-    tokens_home.wait()
-
-
-def attn_back_and_sums(q, k, v, g, delta, lse, segs, tokens, vectors, w_qkv, small, pen, residual, g_out, down, up):
-    L, D = q.shape
-    N, W = 3 * SPLIT, PANEL // SPLIT
-    hbm = pl.BlockSpec(memory_space=pl.ANY)
-    vm = pl.BlockSpec(memory_space=pltpu.VMEM)
-    dma = pltpu.SemaphoreType.DMA
-    shape = jax.ShapeDtypeStruct
-    return pl.pallas_call(
-        back_kernel,
-        out_shape=(shape(down.shape, BF), shape(up.shape, BF), shape((D, 4 * D), BF),
-                   shape((8, L // 8, D), BF), shape(small.shape, F32)),
-        in_specs=[vm] * 11 + [hbm] * 5,
-        out_specs=(hbm,) * 4 + (vm,),
-        scratch_shapes=[
-            pltpu.VMEM((D, L), BF), pltpu.VMEM((D, L), BF), pltpu.VMEM((D, L), F32), pltpu.VMEM((D, L), F32),
-            pltpu.VMEM((BLOCK, L), F32), pltpu.VMEM((2, BLOCK, L), F32), pltpu.VMEM((L, 3 * D), BF),
-            pltpu.VMEM((D, 4 * D), BF), pltpu.VMEM((L, D), BF), pltpu.VMEM((2, BLOCK, D), F32),
-            pltpu.VMEM((N, 2, PANEL, W), BF), pltpu.VMEM((N, 2, PANEL, W), BF), pltpu.VMEM((N, 2, PANEL // 2, W), BF),
-            pltpu.VMEM((N, 2, PANEL // 4, W), BF), pltpu.VMEM((N, 2, 3, PANEL // 16, W), BF),
-            pltpu.VMEM((5,) + small.shape, F32), pltpu.VMEM((5,) + small.shape, F32),
-            dma((N, 24)), dma((N, 24)), dma((N, 4)), dma((7,)), dma((7,)), dma, dma((5,)), dma((5,)),
-            dma((2,)), dma((2,)), dma,
-        ],
-        compiler_params=pltpu.CompilerParams(vmem_limit_bytes=VMEM_LIMIT, collective_id=1, has_side_effects=True),
-        name="attn_back_and_sums",
-    )(q, k, v, g, delta, lse, segs, tokens, vectors, w_qkv, small, pen, residual, g_out, down, up)
 
 
 def front_kernel(tokens_ref, cot_ref, w_ref, vec_ref, seg_ref,
@@ -769,107 +579,317 @@
     return u * half, half + (0.5 * slope) * u * (1.0 - t * t) * (1.0 + 3 * 0.044715 * square)
 
 
-def middle_kernel(att_ref, tok_ref, cot_ref, vec_ref, w_out_ref, w_up_ref, w_down_ref,
-                  output_out, g_ref, res_ref, delta_ref, g_out_ref, g_up_ref, g_down_ref, small_ref,
-                  w_out, w_up, w_down, act, gu, n2t, dyt, gb, out, load, sent, landed, local):
-    L, D = att_ref.shape
-    ff = w_up.shape[1]
+def rest_kernel(att_hbm, tok_hbm, cot_hbm, q_hbm, k_hbm, v_hbm, lse_hbm, pen_hbm, vec_ref, seg_ref,
+                w_qkv_hbm, w_out_hbm, w_up_hbm, w_down_hbm,
+                output_out, tokens_out, down_out, up_out, side_out, small_out, down_part, up_part, out_part, res_part,
+                tok, g, delta, sm_acc, sm_rec, own, from_core, from_one, from_two, from_z,
+                sent, landed, local, home_s, home_r, home_l, sm_s, sm_r, in_s, stage_s, res_s, pen_s):
+    L, D = tok.shape
+    ff = w_up_hbm.shape[1]
+    nb = L // BLOCK
+    width = PANEL // SPLIT
+    pairs = HEADS // 2
     place = Place()
-    place.greet(place.along_cols)
-    loads = [pltpu.make_async_copy(a, b, load.at[i])
-             for i, (a, b) in enumerate(((w_out_ref, w_out), (w_up_ref, w_up), (w_down_ref, w_down)))]
-    for copy in loads:
-        copy.start()
-    small_ref[...] = jnp.zeros_like(small_ref)
-    features = lax.broadcasted_iota(jnp.int32, (D, 128), 0) // HDIM
-    member = jnp.where(features == lax.broadcasted_iota(jnp.int32, (D, 128), 1), 1.0, 0.0).astype(BF)
+    place.greet(place.along_cols + place.along_z)
+    buffers, sems = (own, from_core, from_one, from_two, from_z), (sent, landed, local)
+    chunks = []
+    for source, result, tall in ((down_part, down_out, True), (up_part, up_out, False)):
+        for j in range(SPLIT):
+            chunks.append(Chunk(place, len(chunks), source, result, tall, j * width, buffers, sems))
+    line = Timeline()
     vec = lambda row: vec_ref[row : row + 1, :]
+    sm_acc[0] = jnp.zeros_like(sm_acc[0])
 
     def add_row(row, values):
-        small_ref[row : row + 1, :] += jnp.sum(values, axis=0, keepdims=True)
-
-    for copy in loads:
-        copy.wait()
-
-    def block(b, carry):
-        here = pl.ds(pl.multiple_of(b * ROWS, ROWS), ROWS)
-        att = att_ref[here, :]
-        dy = cot_ref[here, :]
-        residual = tok_ref[here, :].astype(F32) + dot(att, w_out[...]) + vec(ROW_OUT)
-        normal, spread = norm_parts(residual)
-        n2 = (normal * vec(ROW_GAIN2) + vec(ROW_SHIFT2)).astype(BF)
-        n2t[:, here] = n2.T
-        dyt[:, here] = dy.T
-        top = dy.astype(F32)
-        add_row(ROW_DOWN, top)
-        total = residual + vec(ROW_DOWN)
-        grad_two = jnp.zeros((ROWS, D), F32)
-        for j in range(ff // D):
-            part = slice(j * D, (j + 1) * D)
-            value, slope = gelu_pair(dot(n2, w_up[:, part]) + vec(ROW_UP + j))
-            low = value.astype(BF)
-            act[here, part] = low
-            total = total + dot(low, w_down[part, :])
-            grad = (dot(dy, w_down[part, :], NT) * slope).astype(BF)
-            gu[here, part] = grad
-            add_row(ROW_UP + j, grad.astype(F32))
-            grad_two = grad_two + dot(grad, w_up[:, part], NT)
-        out[here, :] = total.astype(BF)
-        add_row(ROW_GAIN2, grad_two * normal)
-        add_row(ROW_SHIFT2, grad_two)
-        grad_residual = top + norm_back(grad_two, normal, spread, vec(ROW_GAIN2))
-        res_ref[here, :] = grad_residual
-        branch = grad_residual.astype(BF)
-        gb[here, :] = branch
-        add_row(ROW_OUT, branch.astype(F32))
-        grad_att = dot(branch, w_out[...], NT).astype(BF)
-        g_ref[here, :] = grad_att
-        product = grad_att.astype(F32) * att.astype(F32)
-        high = product.astype(BF)
-        delta_ref[here, :] = dot(high, member) + dot((product - high.astype(F32)).astype(BF), member)
-        return carry
-
-    lax.fori_loop(0, L // ROWS, block, 0)
-    home = Homeward(place, out, output_out, sent, landed, local)
-    home.start()
-
-    def down(i, carry):
-        part = pl.ds(pl.multiple_of(i * 256, 256), 256)
-        g_down_ref[part, :] = dot(dyt[...], act[:, part]).astype(BF).T
-        return carry
-
-    def up(i, carry):
-        part = pl.ds(pl.multiple_of(i * 256, 256), 256)
-        g_up_ref[:, part] = dot(n2t[...], gu[:, part]).astype(BF)
-        return carry
-
-    lax.fori_loop(0, ff // 256, down, 0)
-    lax.fori_loop(0, ff // 256, up, 0)
-    g_out_ref[...] = dot(att_ref[...], gb[...], ((0,), (0,))).astype(BF)
-    home.wait()
-
-
-def middle(attended, tokens, cotangent, vectors, w_out, w_up, w_down):
+        sm_acc[0, row : row + 1, :] += jnp.sum(values, axis=0, keepdims=True)
+
+    def feed_forward(w_out, w_up, w_down, act, gu, n2t, gb, out, att, cot, res, stage):
+        loads = [pltpu.make_async_copy(a, b, in_s.at[i]) for i, (a, b) in enumerate((
+            (att_hbm, att), (tok_hbm, tok), (w_out_hbm, w_out), (cot_hbm, cot), (w_up_hbm, w_up), (w_down_hbm, w_down)))]
+        for copy in loads:
+            copy.start()
+        features = lax.broadcasted_iota(jnp.int32, (D, 128), 0) // HDIM
+        member = jnp.where(features == lax.broadcasted_iota(jnp.int32, (D, 128), 1), 1.0, 0.0).astype(BF)
+        for copy in loads:
+            copy.wait()
+
+        def forward(b, carry):
+            here = pl.ds(pl.multiple_of(b * ROWS, ROWS), ROWS)
+            dy = cot[here, :]
+            residual = tok[here, :].astype(F32) + dot(att[here, :], w_out[...]) + vec(ROW_OUT)
+            res[here, :] = residual
+            normal, _ = norm_parts(residual)
+            n2 = (normal * vec(ROW_GAIN2) + vec(ROW_SHIFT2)).astype(BF)
+            n2t[:, here] = n2.T
+            add_row(ROW_DOWN, dy.astype(F32))
+            total = residual + vec(ROW_DOWN)
+            for j in range(ff // D):
+                part = slice(j * D, (j + 1) * D)
+                value, slope = gelu_pair(dot(n2, w_up[:, part]) + vec(ROW_UP + j))
+                low = value.astype(BF)
+                act[here, part] = low
+                gu[here, part] = slope.astype(BF)
+                total = total + dot(low, w_down[part, :])
+            out[here, :] = total.astype(BF)
+            return carry
+
+        def backward(b):
+            here = slice(b * ROWS, (b + 1) * ROWS)
+            dy = cot[here, :]
+            normal, spread = norm_parts(res[here, :])
+            grad_two = jnp.zeros((ROWS, D), F32)
+            for j in range(ff // D):
+                part = slice(j * D, (j + 1) * D)
+                grad = (dot(dy, w_down[part, :], NT) * gu[here, part].astype(F32)).astype(BF)
+                gu[here, part] = grad
+                add_row(ROW_UP + j, grad.astype(F32))
+                grad_two = grad_two + dot(grad, w_up[:, part], NT)
+            add_row(ROW_GAIN2, grad_two * normal)
+            add_row(ROW_SHIFT2, grad_two)
+            grad_residual = dy.astype(F32) + norm_back(grad_two, normal, spread, vec(ROW_GAIN2))
+            res[here, :] = grad_residual
+            branch = grad_residual.astype(BF)
+            gb[here, :] = branch
+            add_row(ROW_OUT, branch.astype(F32))
+            grad_att = dot(branch, w_out[...], NT).astype(BF)
+            g[here, :] = grad_att
+            product = grad_att.astype(F32) * att[here, :].astype(F32)
+            high = product.astype(BF)
+            delta[here, :] = dot(high, member) + dot((product - high.astype(F32)).astype(BF), member)
+
+        lax.fori_loop(0, L // ROWS, forward, 0)
+        home = Homeward(place, out, output_out, home_s.at[0], home_r.at[0], home_l.at[0])
+        home.start()
+        line.occupy("plane", 16.0)
+        tiles = ff // 256
+        stored = [pltpu.make_async_copy(stage.at[i % 2], down_part.at[i * 256 : (i + 1) * 256, :], stage_s.at[i % 2])
+                  for i in range(tiles)]
+        for i in range(tiles):
+            if i > 1:
+                stored[i - 2].wait()
+            stage[i % 2] = dot(act[:, i * 256 : (i + 1) * 256], cot[...], ((0,), (0,))).astype(BF)
+            stored[i].start()
+        stored[tiles - 2].wait()
+        stored[tiles - 1].wait()
+        line.worked(6.0)
+        line.begin_all(chunks[:SPLIT])
+        for b in range(L // ROWS):
+            backward(b)
+            line.worked(4.3)
+        tiles = ff // D
+        spread = [pltpu.make_async_copy(w_down.at[i * D : (i + 1) * D, :], up_part.at[:, i * D : (i + 1) * D], stage_s.at[2 + i])
+                  for i in range(tiles)]
+        for i in range(tiles):
+            for j in range(D // 256):
+                w_down[i * D : (i + 1) * D, j * 256 : (j + 1) * 256] = dot(n2t[...], gu[:, i * D + j * 256 : i * D + (j + 1) * 256]).astype(BF)
+            spread[i].start()
+            line.worked(1.6)
+        w_out[...] = dot(att[...], gb[...], ((0,), (0,))).astype(BF)
+        keep = [pltpu.make_async_copy(w_out, out_part, res_s.at[0]), pltpu.make_async_copy(res, res_part, res_s.at[1])]
+        for copy in keep:
+            copy.start()
+        for copy in spread:
+            copy.wait()
+        line.worked(1.5)
+        line.begin_all(chunks[SPLIT:])
+        for copy in keep:
+            copy.wait()
+        home.wait()
+
+    dma = pltpu.SemaphoreType.DMA
+    pl.run_scoped(
+        feed_forward, pltpu.VMEM((D, D), BF), pltpu.VMEM((D, ff), BF), pltpu.VMEM((ff, D), BF), pltpu.VMEM((L, ff), BF),
+        pltpu.VMEM((L, ff), BF), pltpu.VMEM((D, L), BF), pltpu.VMEM((L, D), BF),
+        pltpu.VMEM((L, D), BF), pltpu.VMEM((L, D), BF), pltpu.VMEM((L, D), BF), pltpu.VMEM((L, D), F32),
+        pltpu.VMEM((2, 256, D), BF))
+
+    def attention(q_ref, k_ref, v_ref, lse_ref, w_ref, qt, gt, dkt, dvt, dsum, pen, dqkv, side, gtok, gres):
+        scale = HDIM**-0.5
+        c = scale * LOG2E
+        startr_ref = seg_ref.at[1:2]
+        loads = [pltpu.make_async_copy(a, b, in_s.at[i]) for i, (a, b) in enumerate((
+            (q_hbm, q_ref), (k_hbm, k_ref), (v_hbm, v_ref), (lse_hbm, lse_ref), (w_qkv_hbm, w_ref)))]
+        pen_copies = [pltpu.make_async_copy(pen_hbm.at[b * BLOCK : (b + 1) * BLOCK, :], pen.at[b % 2], pen_s.at[b % 2])
+                      for b in range(nb)]
+        res_copies = [pltpu.make_async_copy(res_part.at[b * BLOCK : (b + 1) * BLOCK, :], gres.at[b % 2], res_s.at[b % 2])
+                      for b in range(nb)]
+        for copy in loads[:4]:
+            copy.start()
+        pen_copies[0].start()
+        loads[4].start()
+        out_copy = pltpu.make_async_copy(out_part, side.at[:, 3 * D : 4 * D], in_s.at[5])
+        out_copy.start()
+        dkt[...] = jnp.zeros_like(dkt)
+        dvt[...] = jnp.zeros_like(dvt)
+        for p in range(pairs):
+            gt[p * 128 : (p + 1) * 128, :] = g[:, p * 128 : (p + 1) * 128].T
+        for copy in loads[:4]:
+            copy.wait()
+        for p in range(pairs):
+            qt[p * 128 : (p + 1) * 128, :] = q_ref[:, p * 128 : (p + 1) * 128].T
+        line.worked(3.0)
+        lower = tri(BLOCK, False)
+        carry = jnp.zeros((1, L), F32)
+        for b in range(nb):
+            i0 = b * BLOCK
+            n = L - i0
+            rowsl = slice(i0, i0 + BLOCK)
+            carry = carry[:, -n:]
+            pen_copies[b].wait()
+            if b + 1 < nb:
+                pen_copies[b + 1].start()
+            pen_b = pen.at[b % 2, :, i0:L]
+
+            def head(p, h):
+                off = p * 128 if isinstance(p, int) else pl.multiple_of(p * 128, 128)
+                q = q_ref[rowsl, pl.ds(off, 128)]
+                gh = g[rowsl, pl.ds(off, 128)]
+                k = k_ref[i0:L, pl.ds(off, 128)]
+                v = v_ref[i0:L, pl.ds(off, 128)]
+                low = lane_low(q.shape)
+                mine = low if h == 0 else jnp.logical_not(low)
+                lane = lax.broadcasted_iota(jnp.int32, (BLOCK, 128), 1)
+                lse = jnp.sum(jnp.where(lane == 2 * p + h, lse_ref[rowsl, :], 0.0), axis=1, keepdims=True)
+                shift = jnp.sum(jnp.where(lane == 2 * p + h, delta[rowsl, :], 0.0), axis=1, keepdims=True)
+                s = dot(jnp.where(mine, q, jnp.zeros_like(q)), k, NT)
+                pr = jnp.exp2(s * c - pen_b[...] - lse)
+                dp = dot(jnp.where(mine, gh, jnp.zeros_like(gh)), v, NT)
+                return s, pr, pr * (dp - shift), off, k
+
+            def finish(p, h, pr, ds, k):
+                base = p * 128 + h * HDIM
+                if not isinstance(p, int):
+                    base = pl.multiple_of(base, 64)
+                dsb = ds.astype(BF)
+                dvt[pl.ds(base, HDIM), i0:L] += dot(gt[pl.ds(base, HDIM), rowsl], pr.astype(BF))
+                dkt[pl.ds(base, HDIM), i0:L] += dot(qt[pl.ds(base, HDIM), rowsl], dsb)
+                return dot(dsb, k)
+
+            def pair(p, carry_):
+                dq = []
+                for h in range(2):
+                    s, pr, ds, off, k = head(p, h)
+                    dsum[:, i0:L] += ds
+                    dq.append(finish(p, h, pr, ds, k))
+                dqkv[rowsl, pl.ds(off, 128)] = (jnp.where(lane_low(dq[0].shape), dq[0], dq[1]) * scale).astype(BF)
+                return carry_
+
+            dsum[:, i0:L] = jnp.zeros((BLOCK, n), F32)
+            each = 0.42 * (nb - b)
+            for begin, end in ((1, 3), (3, pairs)) if b < 2 else ((1, pairs),):
+                lax.fori_loop(begin, end, pair, 0)
+                line.worked(each * (end - begin))
+            s, pr, ds, off, k = head(0, 1)
+            dsum[:, i0:L] += ds
+            dq1 = finish(0, 1, pr, ds, k)
+            s, pr, ds, off, k = head(0, 0)
+            total = dsum[:, i0:L] + ds
+            rows = i0 + lax.broadcasted_iota(jnp.int32, (BLOCK, n), 0)
+            cols = i0 + lax.broadcasted_iota(jnp.int32, (BLOCK, n), 1)
+            picked = (pen_b[...] < 1e29) & (cols > rows) & (startr_ref[0:1, i0:L] == 0) & (s > 0)
+            gsel = (split_sum(lower, total) + carry) * (-8.0 / L)
+            carry = carry + jnp.sum(total, axis=0, keepdims=True)
+            ds = ds + jnp.where(picked, gsel, 0.0)
+            dq0 = finish(0, 0, pr, ds, k)
+            dqkv[rowsl, 0:128] = (jnp.where(lane_low(dq0.shape), dq0, dq1) * scale).astype(BF)
+            line.worked(each * 1.2)
+        for p in range(pairs):
+            sl = slice(p * 128, (p + 1) * 128)
+            dqkv[:, D + p * 128 : D + (p + 1) * 128] = (dkt[sl, :] * scale).T.astype(BF)
+            dqkv[:, 2 * D + p * 128 : 2 * D + (p + 1) * 128] = dvt[sl, :].T.astype(BF)
+
+        def normal_of(b):
+            return norm_parts(tok[b * BLOCK : (b + 1) * BLOCK, :].astype(F32))
+
+        for b in range(nb):
+            normal, _ = normal_of(b)
+            normed = (normal * vec(ROW_GAIN1) + vec(ROW_SHIFT1)).astype(BF)
+            for p in range(pairs):
+                qt[p * 128 : (p + 1) * 128, b * BLOCK : (b + 1) * BLOCK] = normed[:, p * 128 : (p + 1) * 128].T
+        line.worked(3.0)
+        out_copy.wait()
+        for j in range(SPLIT):
+            for panel in range(3):
+                at = slice(panel * D + j * width, panel * D + (j + 1) * width)
+                side[:, at] = dot(qt[...], dqkv[:, at]).astype(BF)
+            line.now += 5.0 / SPLIT
+            line.complete(chunks[j])
+            line.begin(Chunk(place, 2 * SPLIT + j, side, side_out, False, j * width, buffers, sems))
+            line.ready()
+        sm_acc[0, 0:1, :] = jnp.sum(dqkv[:, 0:D].astype(F32), axis=0, keepdims=True)
+        sm_acc[0, 1:2, :] = jnp.sum(dqkv[:, 2 * D : 3 * D].astype(F32), axis=0, keepdims=True)
+        res_copies[0].start()
+        loads[4].wait()
+        g_gain = jnp.zeros((1, D), F32)
+        g_shift = jnp.zeros((1, D), F32)
+        for b in range(nb):
+            rowsl = slice(b * BLOCK, (b + 1) * BLOCK)
+            if b + 1 < nb:
+                res_copies[b + 1].start()
+            normal, spread = normal_of(b)
+            grad = dot(dqkv[rowsl, :], w_ref[...], NT)
+            g_gain = g_gain + jnp.sum(grad * normal, axis=0, keepdims=True)
+            g_shift = g_shift + jnp.sum(grad, axis=0, keepdims=True)
+            back = norm_back(grad, normal, spread, vec(ROW_GAIN1))
+            res_copies[b].wait()
+            gtok[rowsl, :] = (gres[b % 2] + back).astype(BF)
+            line.worked(2.0)
+        tokens_home = Homeward(place, gtok, tokens_out, home_s.at[1], home_r.at[1], home_l.at[1])
+        tokens_home.start()
+        line.occupy("plane", 16.0)
+        sm_acc[0, 3:4, :] = g_gain
+        sm_acc[0, 4:5, :] = g_shift
+        z, col = place.z, place.col
+        friends = [place.core, place.across_x, place.across_y, (z + 1 - 2 * (z % 2), col), (lax.rem(z + 2, 4), col)]
+        smalls = [remote(sm_acc.at[i], sm_rec.at[i], sm_s.at[i], sm_r.at[i], friends[i]) for i in range(5)]
+        smalls[0].start()
+        for i in range(5):
+            line.worked(4.0)
+            smalls[i].wait_recv()
+            following = sm_acc[i] + sm_rec[i]
+            if i < 4:
+                sm_acc[i + 1] = following
+                smalls[i + 1].start()
+            else:
+                small_out[...] = following
+        line.finish()
+        for copy in smalls:
+            copy.wait_send()
+        tokens_home.wait()
+
+    pl.run_scoped(
+        attention, pltpu.VMEM((L, D), BF), pltpu.VMEM((L, D), BF), pltpu.VMEM((L, D), BF), pltpu.VMEM((L, 128), F32),
+        pltpu.VMEM((D, 3 * D), BF), pltpu.VMEM((D, L), BF), pltpu.VMEM((D, L), BF), pltpu.VMEM((D, L), F32),
+        pltpu.VMEM((D, L), F32), pltpu.VMEM((BLOCK, L), F32), pltpu.VMEM((2, BLOCK, L), F32), pltpu.VMEM((L, 3 * D), BF),
+        pltpu.VMEM((D, 4 * D), BF), pltpu.VMEM((L, D), BF), pltpu.VMEM((2, BLOCK, D), F32))
+
+
+def rest(attended, tokens, cotangent, q, k, v, lse, pen, vectors, segs, w_qkv, w_out, w_up, w_down):
     L, D = attended.shape
     ff = w_up.shape[1]
+    N, W = 3 * SPLIT, PANEL // SPLIT
     hbm = pl.BlockSpec(memory_space=pl.ANY)
     vm = pl.BlockSpec(memory_space=pltpu.VMEM)
     dma = pltpu.SemaphoreType.DMA
     shape = jax.ShapeDtypeStruct
+    rows = shape((8, L // 8, D), BF)
+    wide, tall = shape((D, ff), BF), shape((ff, D), BF)
     return pl.pallas_call(
-        middle_kernel,
-        out_shape=(shape((8, L // 8, D), BF), shape((L, D), BF), shape((L, D), F32), shape((L, 128), F32),
-                   shape((D, D), BF), shape((D, ff), BF), shape((ff, D), BF), shape((16, D), F32)),
-        in_specs=[vm] * 4 + [hbm] * 3,
-        out_specs=(hbm,) + (vm,) * 7,
+        rest_kernel,
+        out_shape=(rows, rows, tall, wide, wide, shape((16, D), F32), tall, wide, shape((D, D), BF), shape((L, D), F32)),
+        in_specs=[hbm] * 8 + [vm] * 2 + [hbm] * 4,
+        out_specs=(hbm,) * 5 + (vm,) + (hbm,) * 4,
         scratch_shapes=[
-            pltpu.VMEM((D, D), BF), pltpu.VMEM((D, ff), BF), pltpu.VMEM((ff, D), BF), pltpu.VMEM((L, ff), BF),
-            pltpu.VMEM((L, ff), BF), pltpu.VMEM((D, L), BF), pltpu.VMEM((D, L), BF), pltpu.VMEM((L, D), BF),
-            pltpu.VMEM((L, D), BF), dma((3,)), dma((7,)), dma((7,)), dma,
+            pltpu.VMEM((L, D), BF), pltpu.VMEM((L, D), BF), pltpu.VMEM((L, 128), F32), pltpu.VMEM((5, 16, D), F32),
+            pltpu.VMEM((5, 16, D), F32), pltpu.VMEM((SLOTS, 2, PANEL, W), BF), pltpu.VMEM((SLOTS, 2, PANEL, W), BF),
+            pltpu.VMEM((SLOTS, 2, PANEL // 2, W), BF), pltpu.VMEM((SLOTS, 2, PANEL // 4, W), BF),
+            pltpu.VMEM((SLOTS, 2, 3, PANEL // 16, W), BF),
+            dma((N, 24)), dma((N, 24)), dma((N, 4)), dma((2, 7)), dma((2, 7)), dma((2,)), dma((5,)), dma((5,)),
+            dma((6,)), dma((6,)), dma((2,)), dma((2,)),
         ],
-        compiler_params=pltpu.CompilerParams(vmem_limit_bytes=VMEM_LIMIT, collective_id=3, has_side_effects=True),
-        name="middle",
-    )(attended, tokens, cotangent, vectors, w_out, w_up, w_down)
+        compiler_params=pltpu.CompilerParams(vmem_limit_bytes=VMEM_LIMIT, collective_id=1, has_side_effects=True),
+        name="rest",
+    )(attended, tokens, cotangent, q, k, v, lse, pen, vectors, segs, w_qkv, w_out, w_up, w_down)
 
 
 def summed_grads(grads, copies):

time: 332 us -> 305 us (0.919)
  Pallas kernels: 292 us -> 265 us
    pallas_call x2 -> x1, Pallas kernels: 238 us -> 210 us  [rest(): pl.pallas_call(rest_kernel, out_shape=(rows, rows, tall, wide, wide, shap...]
    unnamed x19 -> x21, local copies, waits for them, and re-layouts: 6.99 us -> 6.7 us
where the time goes in v2:
time: 305 us; the launch traced here: 299 us
  Pallas kernels  265 us (87%)
  other arithmetic  21.7 us (7%)
  local copies, waits for them, and re-layouts  11.9 us (4%)
    pallas_call x1, Pallas kernels, rest(): pl.pallas_call(rest_kernel, out_shape=(rows, rows, tall, wide, wide, shap...  210 us
    pallas_call x1, Pallas kernels, front(): pl.pallas_call(front_kernel, out_shape=(rows,) * 6 + (jax.ShapeDtypeStruc...  54.2 us
    unnamed x21, local copies, waits for them, and re-layouts  6.7 us

profile of v2, /device:TPU:0, one launch (start us, length us, event | category | flops | bytes accessed | tf_op | source)
XLA Modules:
  0.0 299.1 jit_solution(586520705405021362)
XLA Ops:
  0.7 0.9 compare_reduce_fusion
  1.6 0.1 add_convert_fusion
  1.7 0.8 constant_dynamic-slice_fusion
  2.4 0.6 pad_add_fusion.seg_ref
  3.0 0.7 constant_dynamic-update-slice_fusion.8
  3.7 0.7 constant_dynamic-update-slice_fusion.7
  4.4 0.7 constant_dynamic-update-slice_fusion.6
  5.1 0.7 constant_dynamic-update-slice_fusion.5
  5.8 0.7 constant_dynamic-update-slice_fusion.4
  6.5 0.7 constant_dynamic-update-slice_fusion.3
  7.2 0.7 constant_dynamic-update-slice_fusion.2
  7.9 0.7 constant_dynamic-update-slice_fusion.1
  8.6 0.7 constant_dynamic-update-slice_fusion
  9.3 0.6 reshape.41.vec_ref
  9.9 54.2 %front.1 = (bf16[1024,768]{1,0:T(8,128)(2,1)}, bf16[1024,768]{1,0:T(8,128)(2,1)}, bf16[1024,768]{1,0:T(8,128)(2,1)}, bf16[1024,768]{1,0:T(8,128)(2,1)}, bf16[102...) custom-call(bf16[8,128,768]{2,1,0:T(8,128)(2,1)} %tokens_ref.1, ...), custom_call_target="tpu_custom_call" | custom-call | tf_op jit(solution)/shard_map/front/pallas_call | solution.py:560
  64.1 210.5 %rest.1 = (bf16[8,128,768]{2,1,0:T(8,128)(2,1)}, bf16[8,128,768]{2,1,0:T(8,128)(2,1)}, bf16[3072,768]{1,0:T(8,128)(2,1)}, bf16[768,3072]{1,0:T(8,128)(2,1)}, bf1...) custom-call(bf16[1024,768]{1,0:T(8,128)(2,1)} %get-tuple-element.29., ...), custom_call_target="tpu_custom_call" | custom-call | tf_op jit(solution)/shard_map/rest/pallas_call | solution.py:877
  274.6 0.7 slice.52
  275.3 1.7 slice_reduce_fusion
  277.0 0.6 reshape.42
  277.6 0.0 slice-start.2
  277.6 3.0 %slice_convert_fusion.1 = f32[768,768]{1,0:T(8,128)} fusion(bf16[768,3072]{1,0:T(8,128)(2,1)} %get-tuple-element.39), kind=kLoop, calls=%fused_computation.1 | loop fusion | flops 589824 | bytes 3538944 | tf_op jit(solution)/shard_map/convert_element_type | solution.py:923
  280.6 0.0 copy-start.1
  280.6 0.0 slice-start.3
  280.6 5.6 %slice_convert_fusion = f32[768,2304]{1,0:T(8,128)} fusion(bf16[768,3072]{1,0:T(8,128)(2,1)} %get-tuple-element.39), kind=kLoop, calls=%fused_computation | loop fusion | flops 1769472 | bytes 10616832 | tf_op jit(solution)/shard_map/convert_element_type | solution.py:922
  286.3 0.0 copy-done.1
  286.3 0.0 slice-start
  286.3 1.9 convert_element_type.20
  288.2 0.0 slice-done.2
  288.2 0.0 slice-done.3
  288.2 0.0 slice-start.1
  288.2 5.0 %convert_element_type.23 = f32[768,3072]{1,0:T(8,128)} convert(bf16[768,3072]{1,0:T(8,128)(2,1)S(1)} %bitcast.4) | non-fusion elementwise | flops 2359296 | bytes 14155776 | tf_op jit(solution)/shard_map/convert_element_type | solution.py:924
  293.3 0.0 slice-done
  293.3 0.0 slice-done.1
  293.3 0.0 copy-start
  293.3 4.5 %convert_element_type.24 = f32[3072,768]{1,0:T(8,128)} convert(bf16[3072,768]{1,0:T(8,128)(2,1)S(1)} %bitcast.2) | non-fusion elementwise | flops 2359296 | bytes 14155776 | tf_op jit(solution)/shard_map/convert_element_type | solution.py:924
  297.8 0.0 copy-done
  297.8 1.1 copy.41
  (3 shorter events, 0.0 us)
Async XLA Ops:
  277.6 10.6 %slice-start.2 = ((s8[4718592]{0:T(1024)(128)(4,1)}), s8[4194304]{0:T(1024)(128)(4,1)S(1)}, s32[]{:S(2)}) async-start(s8[4718592]{0:T(1024)(128)(4,1)} %bitcast.3), calls=%async_computation.2 | async-start | bytes 8388608
  280.6 5.6 %copy-start.1 = (bf16[8,128,768]{2,1,0:T(8,128)(2,1)S(1)}, bf16[8,128,768]{2,1,0:T(8,128)(2,1)}, u32[]{:S(2)}) copy-start(bf16[8,128,768]{2,1,0:T(8,128)(2,1)} %get-tuple-element.38) | copy-start | bytes 4718596
  280.6 7.6 %slice-start.3 = ((s8[4718592]{0:T(1024)(128)(4,1)}), s8[524288]{0:T(1024)(128)(4,1)S(1)}, s32[]{:S(2)}) async-start(s8[4718592]{0:T(1024)(128)(4,1)} %bitcast.3), calls=%async_computation.3 | async-start | bytes 1048576
  286.3 7.0 %slice-start = ((s8[4718592]{0:T(1024)(128)(4,1)}), s8[4194304]{0:T(1024)(128)(4,1)S(1)}, s32[]{:S(2)}) async-start(s8[4718592]{0:T(1024)(128)(4,1)} %bitcast.1), calls=%async_computation | async-start | bytes 8388608
  288.2 5.1 %slice-start.1 = ((s8[4718592]{0:T(1024)(128)(4,1)}), s8[524288]{0:T(1024)(128)(4,1)S(1)}, s32[]{:S(2)}) async-start(s8[4718592]{0:T(1024)(128)(4,1)} %bitcast.1), calls=%async_computation.1 | async-start | bytes 1048576
  293.3 4.5 %copy-start = (bf16[8,128,768]{2,1,0:T(8,128)(2,1)S(1)}, bf16[8,128,768]{2,1,0:T(8,128)(2,1)}, u32[]{:S(2)}) copy-start(bf16[8,128,768]{2,1,0:T(8,128)(2,1)} %get-tuple-element.66) | copy-start | bytes 4718596
